TPU v7x, 32 devices: a whole 2x2x4 slice. The times are simulated.
32 devices in a mesh: dp: 8 (over y, x, core), head: 4 (over z).
Axes of the slice: x: 2, y: 2, z: 4, core: 2. Of those that a mesh axis runs over, the one named last changes fastest.
Arguments:
- tokens: bfloat16 [32768, 256], P(('dp', 'head')), may hold values from -6 to 6
- lengths: int32 [128], P('dp'), may hold values from 32 to 256, as said below
- cotangent: bfloat16 [32768, 256], P(('dp', 'head')), may hold values from -6 to 6
- gain_attn: float32 [2, 256], replicated, may hold values from 0.1 to 1.9
- gain_mlp: float32 [2, 256], replicated, may hold values from 0.1 to 1.9
- w_qkv: bfloat16 [2, 256, 3, 256], P(None, None, None, 'head'), may hold values from -4 to 4, as said below
- w_out: bfloat16 [2, 256, 256], P(None, 'head'), may hold values from -4 to 4, as said below
- w_up: bfloat16 [2, 256, 1024], P(None, None, 'head'), may hold values from -4 to 4, as said below
- w_down: bfloat16 [2, 1024, 256], P(None, 'head'), may hold values from -0.1875 to 0.1875
- w_cross: bfloat16 [2, 256, 256], P(None, None, 'head'), may hold values from -4 to 4, as said below
- b_cross: bfloat16 [2, 256], P(None, 'head'), may hold values from -1 to 1, as said below
Outputs:
- output: float32 [32768, 256], P(('dp', 'head'))
- grad_tokens: float32 [32768, 256], P(('dp', 'head'))
- grad_gain_attn: float32 [2, 256], replicated
- grad_gain_mlp: float32 [2, 256], replicated
- grad_w_qkv: float32 [2, 256, 3, 256], P(None, None, None, 'head')
- grad_w_out: float32 [2, 256, 256], P(None, 'head')
- grad_w_up: float32 [2, 256, 1024], P(None, None, 'head')
- grad_w_down: float32 [2, 1024, 256], P(None, 'head')
- grad_w_cross: float32 [2, 256, 256], P(None, None, 'head')
- grad_b_cross: float32 [2, 256], P(None, 'head')
Inputs may be any that keep to these rules, and one draw needn't show every extreme that they name: lengths[b] slots of sample b are present and the rest are absent; some sample has exactly 256 and some exactly 32. `w_qkv`: independent entries with deviation about 1 / sqrt(128). `w_out`: independent entries with deviation about 1 / sqrt(16). `w_up`: independent entries with deviation about 1 / sqrt(256). `w_cross`: independent entries with deviation about 1 / sqrt(1024). `b_cross`: independent entries with deviation about 0.25.
All inputs are finite; a program needn't handle non-finite values.
Results may differ from a plain program's by a relative error of at most 0.019.
The roundings to bfloat16 on the way count: a program that leaves them out, or rounds other values in their place, can miss the bound.
Values may be sent and summed in bfloat16 or wider, within the bound.
No kernel may reach another device: no remote copies, remote signals or barrier semaphores. Data moves between devices by JAX's collectives and lax.ppermute only.
A program may use at most 128 MiB of HBM per device.

v0:
```python
import jax
import jax.numpy as jnp
from jax import lax
from jax.sharding import PartitionSpec as P

HD = 64
LAYERS = 2


EPSILON = 1e-06
MASKED_SCORE = -1000000000.0


def gelu_exact(values):
    return jax.nn.gelu(values, approximate=False)


def norm_rows(values, gain):
    rescale = lax.rsqrt(jnp.mean(values * values, axis=-1, keepdims=True) + EPSILON)
    return (values * rescale * gain, rescale)


def norm_back(values, rescale, gain, gradient):
    scaled = gradient * gain
    product_mean = jnp.mean(values * scaled, axis=-1, keepdims=True)
    grad_values = rescale * scaled - values * (rescale * rescale * rescale) * product_mean
    return (grad_values, jnp.sum(gradient * values * rescale, axis=0))


def masked_scores(query_rows, key_rows, lengths_blk):
    logits = jnp.einsum("bqhd,bkhd->bhqk", query_rows, key_rows, preferred_element_type=jnp.float32)
    logits = logits * query_rows.shape[3] ** (-0.5)
    slot_ids = lax.broadcasted_iota(jnp.int32, logits.shape, 3)
    return jnp.where(slot_ids < lengths_blk[:, None, None, None], logits, MASKED_SCORE)


def attend_block(operands):
    blocked, lengths_blk = operands
    logits = masked_scores(blocked[:, :, 0], blocked[:, :, 1], lengths_blk)
    row_max = jnp.max(logits, axis=-1, keepdims=True)
    exponent = jnp.exp(logits - row_max)
    row_total = jnp.sum(exponent, axis=-1, keepdims=True)
    probability = (exponent / row_total).astype(jnp.bfloat16)
    attn_mix = jnp.einsum(
        "bhqk,bkhd->bqhd", probability, blocked[:, :, 2], preferred_element_type=jnp.float32
    )
    return (attn_mix.astype(jnp.bfloat16), (row_max + jnp.log(row_total))[..., 0])


def attend_back_block(operands):
    blocked, lengths_blk, logsum, grad_out = operands
    query_rows = blocked[:, :, 0]
    key_rows = blocked[:, :, 1]
    value_rows = blocked[:, :, 2]
    logits = masked_scores(query_rows, key_rows, lengths_blk)
    probability = jnp.exp(logits - logsum[..., None])
    grad_values = jnp.einsum(
        "bhqk,bqhd->bkhd",
        probability.astype(jnp.bfloat16),
        grad_out,
        preferred_element_type=jnp.float32,
    )
    grad_probs = jnp.einsum(
        "bqhd,bkhd->bhqk", grad_out, value_rows, preferred_element_type=jnp.float32
    )
    row_dot = jnp.sum(grad_probs * probability, axis=-1, keepdims=True)
    grad_logits = (probability * (grad_probs - row_dot)).astype(jnp.bfloat16)
    factor = query_rows.shape[3] ** (-0.5)
    grad_query = (
        jnp.einsum("bhqk,bkhd->bqhd", grad_logits, key_rows, preferred_element_type=jnp.float32)
        * factor
    )
    grad_keys = (
        jnp.einsum("bhqk,bqhd->bkhd", grad_logits, query_rows, preferred_element_type=jnp.float32)
        * factor
    )
    return jnp.stack([grad_query, grad_keys, grad_values], axis=2).astype(jnp.bfloat16)


def attention(qkv, lengths_here):
    row_count, head_count, head_dim = (qkv.shape[0], qkv.shape[2], qkv.shape[3])
    seq_len = row_count // lengths_here.shape[0]
    blocked = qkv.reshape(row_count // (2 * seq_len), 2, seq_len, 3, head_count, head_dim)
    attn_mix, logsum = lax.map(attend_block, (blocked, lengths_here.reshape(-1, 2)))
    return (attn_mix.reshape(row_count, head_count * head_dim), logsum)


def attention_back(qkv, lengths_here, logsum, grad_mix):
    row_count, head_count, head_dim = (qkv.shape[0], qkv.shape[2], qkv.shape[3])
    seq_len = row_count // lengths_here.shape[0]
    blocked = qkv.reshape(row_count // (2 * seq_len), 2, seq_len, 3, head_count, head_dim)
    grad_blocks = grad_mix.reshape(row_count // (2 * seq_len), 2, seq_len, head_count, head_dim)
    grad_qkv = lax.map(
        attend_back_block, (blocked, lengths_here.reshape(-1, 2), logsum, grad_blocks)
    )
    return grad_qkv.reshape(row_count, 3, head_count * head_dim)


def forward_layer(current, lengths_here, attn_gain, feed_gain, weights):
    w_qkv_l, w_out_l, w_up_l, w_down_l, w_cross_l, b_cross_l = weights
    normed, rescale_one = norm_rows(current, attn_gain)
    normed = normed.astype(jnp.bfloat16)
    gathered = lax.all_gather(normed, "head", axis=0, tiled=True)
    row_count = gathered.shape[0]
    qkv = jnp.einsum("rd,dtc->rtc", gathered, w_qkv_l, preferred_element_type=jnp.float32).astype(
        jnp.bfloat16
    )
    qkv = qkv.reshape(row_count, 3, qkv.shape[2] // HD, HD)
    cross_cols = jnp.dot(
        gathered, w_cross_l, preferred_element_type=jnp.float32
    ) + b_cross_l.astype(jnp.float32)
    cross_gate = lax.all_to_all(cross_cols, "head", split_axis=0, concat_axis=1, tiled=True)
    attn_mix, logsum = attention(qkv, lengths_here)
    attended = lax.psum_scatter(
        jnp.dot(attn_mix, w_out_l, preferred_element_type=jnp.float32),
        "head",
        scatter_dimension=0,
        tiled=True,
    )
    middle = current + attended
    normed_two, rescale_two = norm_rows(middle, feed_gain)
    normed_two = normed_two.astype(jnp.bfloat16)
    gathered_two = lax.all_gather(normed_two, "head", axis=0, tiled=True)
    pre_act = jnp.dot(gathered_two, w_up_l, preferred_element_type=jnp.float32)
    hidden = gelu_exact(pre_act).astype(jnp.bfloat16)
    feed_out = lax.psum_scatter(
        jnp.dot(hidden, w_down_l, preferred_element_type=jnp.float32),
        "head",
        scatter_dimension=0,
        tiled=True,
    )
    result = middle + feed_out + current * cross_gate
    saved_vals = (
        current,
        rescale_one,
        gathered,
        qkv,
        logsum,
        attn_mix,
        cross_gate,
        middle,
        rescale_two,
        gathered_two,
        pre_act,
        hidden,
    )
    return (result, saved_vals)


def backward_layer(gradient, lengths_here, attn_gain, feed_gain, weights, saved_vals):
    w_qkv_l, w_out_l, w_up_l, w_down_l, w_cross_l, b_cross_l = weights
    (
        current,
        rescale_one,
        gathered,
        qkv,
        logsum,
        attn_mix,
        cross_gate,
        middle,
        rescale_two,
        gathered_two,
        pre_act,
        hidden,
    ) = saved_vals
    grad_cross = (gradient * current).astype(jnp.bfloat16)
    grad_input = gradient * cross_gate
    grad_feed = gradient.astype(jnp.bfloat16)
    feed_rows = lax.all_gather(grad_feed, "head", axis=0, tiled=True)
    grad_down = jnp.einsum("rf,rd->fd", hidden, feed_rows, preferred_element_type=jnp.float32)
    grad_hidden = jnp.einsum("rd,fd->rf", feed_rows, w_down_l, preferred_element_type=jnp.float32)
    grad_pre = jax.vjp(gelu_exact, pre_act)[1](grad_hidden)[0].astype(jnp.bfloat16)
    grad_up = jnp.einsum("rd,rf->df", gathered_two, grad_pre, preferred_element_type=jnp.float32)
    grad_normed_two = lax.psum_scatter(
        jnp.einsum("rf,df->rd", grad_pre, w_up_l, preferred_element_type=jnp.float32),
        "head",
        scatter_dimension=0,
        tiled=True,
    )
    grad_middle, grad_feed_gain = norm_back(middle, rescale_two, feed_gain, grad_normed_two)
    grad_middle = grad_middle + gradient
    grad_input = grad_input + grad_middle
    grad_attn = grad_middle.astype(jnp.bfloat16)
    attn_rows = lax.all_gather(grad_attn, "head", axis=0, tiled=True)
    grad_out = jnp.einsum("rc,rd->cd", attn_mix, attn_rows, preferred_element_type=jnp.float32)
    grad_mix = jnp.einsum(
        "rd,cd->rc", attn_rows, w_out_l, preferred_element_type=jnp.float32
    ).astype(jnp.bfloat16)
    grad_flat = attention_back(qkv, lengths_here, logsum, grad_mix)
    grad_qkv_w = jnp.einsum("rd,rtc->dtc", gathered, grad_flat, preferred_element_type=jnp.float32)
    cross_cols = lax.all_to_all(grad_cross, "head", split_axis=1, concat_axis=0, tiled=True)
    grad_cross_w = jnp.einsum("rd,rc->dc", gathered, cross_cols, preferred_element_type=jnp.float32)
    grad_bias = jnp.sum(cross_cols.astype(jnp.float32), axis=0)
    from_qkv = jnp.einsum("rtc,dtc->rd", grad_flat, w_qkv_l, preferred_element_type=jnp.float32)
    grad_normed = lax.psum_scatter(
        from_qkv
        + jnp.einsum("rc,dc->rd", cross_cols, w_cross_l, preferred_element_type=jnp.float32),
        "head",
        scatter_dimension=0,
        tiled=True,
    )
    grad_current, grad_attn_gain = norm_back(current, rescale_one, attn_gain, grad_normed)
    grad_input = grad_input + grad_current
    layer_grads = (grad_qkv_w, grad_out, grad_up, grad_down, grad_cross_w, grad_bias)
    return (grad_input, layer_grads, grad_attn_gain, grad_feed_gain)


def body(
    tokens, lengths, cotangent, gain_attn, gain_mlp, w_qkv, w_out, w_up, w_down, w_cross, b_cross
):
    current = tokens.astype(jnp.float32)
    layer_weights = []
    layer_saved = []
    for layer_num in range(LAYERS):
        weights = (
            w_qkv[layer_num],
            w_out[layer_num],
            w_up[layer_num],
            w_down[layer_num],
            w_cross[layer_num],
            b_cross[layer_num],
        )
        current, saved_vals = forward_layer(
            current, lengths, gain_attn[layer_num], gain_mlp[layer_num], weights
        )
        layer_weights.append(weights)
        layer_saved.append(saved_vals)
    gradient = cotangent.astype(jnp.float32)
    grad_list = [None] * LAYERS
    for layer_num in range(LAYERS - 1, -1, -1):
        gradient, layer_grads, grad_attn_gain, grad_feed_gain = backward_layer(
            gradient,
            lengths,
            gain_attn[layer_num],
            gain_mlp[layer_num],
            layer_weights[layer_num],
            layer_saved[layer_num],
        )
        grad_qkv_w, grad_out, grad_up, grad_down, grad_cross_w, grad_bias = layer_grads
        grad_list[layer_num] = lax.psum(
            (
                grad_qkv_w,
                grad_out,
                grad_up,
                grad_down,
                grad_cross_w,
                grad_bias,
                grad_attn_gain,
                grad_feed_gain,
            ),
            "dp",
        )
    stacked = [
        jnp.stack([grad_list[layer_num][member] for layer_num in range(LAYERS)])
        for member in range(8)
    ]
    attn_gain_grad, feed_gain_grad = lax.psum((stacked[6], stacked[7]), "head")
    return (
        current,
        gradient,
        attn_gain_grad,
        feed_gain_grad,
        stacked[0],
        stacked[1],
        stacked[2],
        stacked[3],
        stacked[4],
        stacked[5],
    )


def solution(mesh):
    return jax.shard_map(
        body,
        mesh=mesh,
        in_specs=(
            P(("dp", "head"), None),
            P("dp"),
            P(("dp", "head"), None),
            P(),
            P(),
            P(None, None, None, "head"),
            P(None, "head", None),
            P(None, None, "head"),
            P(None, "head", None),
            P(None, None, "head"),
            P(None, "head"),
        ),
        out_specs=(
            P(("dp", "head"), None),
            P(("dp", "head"), None),
            P(),
            P(),
            P(None, None, None, "head"),
            P(None, "head", None),
            P(None, None, "head"),
            P(None, "head", None),
            P(None, None, "head"),
            P(None, "head"),
        ),
        check_vma=False,
    )
```

profile of v0, /device:TPU:9, one launch (start us, length us, event | category | flops | bytes accessed | tf_op | source)
XLA Modules:
  0.0 1367.7 jit_solution(8121680842432584534)
XLA Ops:
  13.7 43.6 %all-gather.9.cloned.1.call-done = bf16[4096,256]{1,0:T(8,128)(2,1)} async-done(((bf16[1024,256]{1,0:T(8,128)(2,1)}), bf16[4096,256]{1,0:T(8,128)(2,1)}) %all-gather.9.cloned.1.call-update) | async-done | bytes 2097168 | tf_op jit(solution)/shard_map/all_gather | solution.py:103
  64.6 6.3 while.44
  71.9 2.7 fusion.94
  74.8 77.4 %reduce-scatter.9.cloned.1.call-done = f32[1024,256]{1,0:T(8,128)} async-done(((f32[4096,256]{1,0:T(8,128)}), f32[1024,256]{1,0:T(8,128)}) %reduce-scatter.9.cloned.1.call-update) | async-done | bytes 1048592 | tf_op jit(solution)/shard_map/reduce_scatter | solution.py:114
  156.6 44.6 %all-gather.11.cloned.1.call-done = bf16[4096,256]{1,0:T(8,128)(2,1)} async-done(((bf16[1024,256]{1,0:T(8,128)(2,1)}), bf16[4096,256]{1,0:T(8,128)(2,1)}) %all-gather.11.cloned.1.call-update) | async-done | bytes 2097168 | tf_op jit(solution)/shard_map/all_gather | solution.py:123
  201.2 12.1 multiply_convert_fusion.3
  214.7 2.7 fusion.68
  220.7 56.1 %all_to_all.76 = f32[4,1024,64]{1,2,0:T(8,128)} all-to-all(f32[4,1024,64]{1,2,0:T(8,128)S(1)} %bitcast.423), channel_id=1, replica_groups=mesh['dp'=8,'head'=4] {'head'}, dimensions={0} | all-to-all | bytes 2097152 | tf_op jit(solution)/shard_map/all_to_all | solution.py:112
  276.8 2.5 copy.48
  279.3 38.2 %reduce-scatter.11.cloned.1.call-done = f32[1024,256]{1,0:T(8,128)} async-done(((f32[4096,256]{1,0:T(8,128)}), f32[1024,256]{1,0:T(8,128)}) %reduce-scatter.11.cloned.1.call-update) | async-done | bytes 1048592 | tf_op jit(solution)/shard_map/reduce_scatter | solution.py:126
  317.5 2.9 fusion.44
  322.6 43.0 %all-gather.13.cloned.1.call-done = bf16[4096,256]{1,0:T(8,128)(2,1)} async-done(((bf16[1024,256]{1,0:T(8,128)(2,1)}), bf16[4096,256]{1,0:T(8,128)(2,1)}) %all-gather.13.cloned.1.call-update) | async-done | bytes 2097168 | tf_op jit(solution)/shard_map/all_gather | solution.py:103
  365.6 2.4 fusion.118
  369.4 3.8 reshape_reshape.9
  373.3 3.1 copy.49
  376.6 13.7 while.45
  392.5 2.8 fusion.89
  395.4 77.5 %reduce-scatter.13.cloned.1.call-done = f32[1024,256]{1,0:T(8,128)} async-done(((f32[4096,256]{1,0:T(8,128)}), f32[1024,256]{1,0:T(8,128)}) %reduce-scatter.13.cloned.1.call-update) | async-done | bytes 1048592 | tf_op jit(solution)/shard_map/reduce_scatter | solution.py:114
  477.5 43.9 %all-gather.15.cloned.1.call-done = bf16[4096,256]{1,0:T(8,128)(2,1)} async-done(((bf16[1024,256]{1,0:T(8,128)(2,1)}), bf16[4096,256]{1,0:T(8,128)(2,1)}) %all-gather.15.cloned.1.call-update) | async-done | bytes 2097168 | tf_op jit(solution)/shard_map/all_gather | solution.py:123
  521.4 12.3 multiply_convert_fusion.2
  533.7 34.0 %all-gather.17.cloned.1.call-done = bf16[4096,256]{1,0:T(8,128)(2,1)} async-done(((bf16[1024,256]{1,0:T(8,128)(2,1)}), bf16[4096,256]{1,0:T(8,128)(2,1)}) %all-gather.17.cloned.1.call-update) | async-done | bytes 2097168 | tf_op jit(solution)/shard_map/all_gather | solution.py:169
  567.7 5.9 add_convert_fusion.1
  575.0 2.8 fusion.62
  577.8 77.4 %reduce-scatter.17.cloned.1.call-done = f32[1024,256]{1,0:T(8,128)} async-done(((f32[4096,256]{1,0:T(8,128)}), f32[1024,256]{1,0:T(8,128)}) %reduce-scatter.17.cloned.1.call-update) | async-done | bytes 1048592 | tf_op jit(solution)/shard_map/reduce_scatter | solution.py:174
  657.2 2.8 fusion.106
  662.1 4.3 all-to-all-start.2
  666.6 17.1 %all-to-all-done.2 = bf16[1024,4,64]{0,2,1:T(8,128)(2,1)} async-done(((bf16[1024,4,64]{0,2,1:T(8,128)(2,1)}), bf16[1024,4,64]{0,2,1:T(8,128)(2,1)}, u32[]{:S(2)}, u32[]{:S(2)}) %all-to-all-start.2) | async-done | bytes 524320 | tf_op jit(solution)/shard_map/all_to_all | solution.py:191
  685.7 26.7 %all-gather.19.cloned.1.call-done = bf16[4096,256]{1,0:T(8,128)(2,1)} async-done(((bf16[1024,256]{1,0:T(8,128)(2,1)}), bf16[4096,256]{1,0:T(8,128)(2,1)}) %all-gather.19.cloned.1.call-update) | async-done | bytes 2097168 | tf_op jit(solution)/shard_map/all_gather | solution.py:184
  712.4 3.1 convolution_convert_fusion.5
  719.8 32.9 %while.46 = (s32[]{:T(128)}, bf16[8,2,256,3,1,64]{2,1,0,5,3,4:T(2,128)(2,1)}, bf16[8,2,256,3,1,64]{2,5,1,3,4,0:T(8,128)(2,1)}, s32[8,2]{1,0:T(8,128)S(1)}, f32[8...) while((s32[]{:T(128)}, bf16[8,2,256,3,1,64]{2,1,0,5,3,4:T(2,128)(2,1)}, ...), condition=%wide.region_20.21_spmd, body=%wide.region_18.20_spmd.sunk | while | flops 85556736 | bytes 5909613 | solution.py:93
  752.7 3.8 reshape.510
  758.8 2.8 convolution_add_fusion.1
  761.7 4.2 fusion.58
  768.4 59.1 %all_to_all.77 = f32[4,1024,64]{1,2,0:T(8,128)} all-to-all(f32[4,1024,64]{1,2,0:T(8,128)S(1)} %bitcast.426), channel_id=1, replica_groups=mesh['dp'=8,'head'=4] {'head'}, dimensions={0} | all-to-all | bytes 2097152 | tf_op jit(solution)/shard_map/all_to_all | solution.py:112
  827.5 2.6 copy.52
  830.1 32.8 %reduce-scatter.19.cloned.1.call-done = f32[1024,256]{1,0:T(8,128)} async-done(((f32[4096,256]{1,0:T(8,128)}), f32[1024,256]{1,0:T(8,128)}) %reduce-scatter.19.cloned.1.call-update) | async-done | bytes 1048592 | tf_op jit(solution)/shard_map/reduce_scatter | solution.py:195
  864.9 76.2 %reduce-scatter.15.cloned.1.call-done = f32[1024,256]{1,0:T(8,128)} async-done(((f32[4096,256]{1,0:T(8,128)}), f32[1024,256]{1,0:T(8,128)}) %reduce-scatter.15.cloned.1.call-update) | async-done | bytes 1048592 | tf_op jit(solution)/shard_map/reduce_scatter | solution.py:126
  941.1 4.3 fusion.49
  947.2 44.6 %all-gather.21.cloned.1.call-done = bf16[4096,256]{1,0:T(8,128)(2,1)} async-done(((bf16[1024,256]{1,0:T(8,128)(2,1)}), bf16[4096,256]{1,0:T(8,128)(2,1)}) %all-gather.21.cloned.1.call-update) | async-done | bytes 2097168 | tf_op jit(solution)/shard_map/all_gather | solution.py:169
  991.8 6.0 add_convert_fusion
  999.2 2.7 fusion.72
  1002.0 77.5 %reduce-scatter.21.cloned.1.call-done = f32[1024,256]{1,0:T(8,128)} async-done(((f32[4096,256]{1,0:T(8,128)}), f32[1024,256]{1,0:T(8,128)}) %reduce-scatter.21.cloned.1.call-update) | async-done | bytes 1048592 | tf_op jit(solution)/shard_map/reduce_scatter | solution.py:174
  1081.5 3.1 fusion.107
  1084.7 2.7 convolution_bitcast_fusion.6
  1087.3 3.7 convolution_bitcast_fusion.4
  1092.1 4.6 all-to-all-start.3
  1096.7 3.7 convolution_bitcast_fusion.2
  1100.5 3.8 reshape.523
  1104.3 2.7 convolution_bitcast_fusion.8
  1107.0 3.4 fusion.120
  1110.3 11.7 all-to-all-done.3
  1125.0 3.7 convolution_bitcast_fusion.3
  1130.2 8.8 all-gather.23.cloned.1.call-done
  1144.7 38.0 %while.47 = (s32[]{:T(128)}, bf16[8,2,256,3,1,64]{2,1,0,5,3,4:T(2,128)(2,1)}, bf16[8,2,256,3,1,64]{2,5,1,3,4,0:T(8,128)(2,1)}, s32[8,2]{1,0:T(8,128)S(1)}, f32[8...) while((s32[]{:T(128)}, bf16[8,2,256,3,1,64]{2,1,0,5,3,4:T(2,128)(2,1)}, ...), condition=%wide.region_27.28_spmd, body=%wide.region_25.27_spmd.sunk | while | flops 85556736 | bytes 5909613 | solution.py:93
  1182.7 3.8 reshape.521
  1186.5 2.7 convolution_bitcast_fusion.9
  1189.2 2.7 fusion.119
  1192.0 2.9 reshape.512
  1195.9 2.7 convolution_add_fusion
  1201.3 54.2 %all-reduce.5.cloned.1.call-done = (f32[1,256,3,64]{1,3,2,0:T(8,128)}, f32[1,256,3,64]{1,3,2,0:T(8,128)}, f32[1,64,256]{2,1,0:T(8,128)}, f32[1,64,256]{2,1,0:T(8...) async-done(((f32[1,256,3,64]{1,3,2,0:T(8,128)}, ...) | async-done | bytes 1703952 | tf_op jit(solution)/shard_map/psum | solution.py:240
  1262.6 72.3 %reduce-scatter.23.cloned.1.call-done = f32[1024,256]{1,0:T(8,128)} async-done(((f32[4096,256]{1,0:T(8,128)}), f32[1024,256]{1,0:T(8,128)}) %reduce-scatter.23.cloned.1.call-update) | async-done | bytes 1048592 | tf_op jit(solution)/shard_map/reduce_scatter | solution.py:195
  1336.8 12.0 all-reduce
  1349.3 8.1 all-reduce.2
  1357.4 3.3 fusion.52
  (494 shorter events, 172.1 us)
Async XLA Ops:
  7.2 50.1 %all-gather.9.cloned.1.call-start = ((), (), s32[]{:S(2)}) async-start(), calls=%async_computation.12 | async-start | bytes 2621440 | tf_op jit(solution)/shard_map/all_gather | solution.py:103
  9.1 3.6 copy-start.35
  9.9 2.9 copy-start.41
  11.9 140.3 %reduce-scatter.9.cloned.1.call-start = ((), (), s32[]{:S(2)}) async-start(), calls=%async_computation.13 | async-start | bytes 5242880 | tf_op jit(solution)/shard_map/reduce_scatter | solution.py:114
  64.5 7.3 copy-start.29
  71.5 3.2 copy-start.9
  71.9 2.8 copy-start.14
  71.9 2.8 copy-start.44
  71.9 80.3 %copy-start = (bf16[1024,256]{1,0:T(8,128)(2,1)S(1)}, bf16[1024,256]{1,0:T(8,128)(2,1)}, u32[]{:S(2)}) copy-start(bf16[1024,256]{1,0:T(8,128)(2,1)} %param.19) | copy-start | bytes 1572868
  74.6 126.6 %copy-start.25 = (bf16[2,256,256]{2,1,0:T(8,128)(2,1)S(1)}, bf16[2,256,256]{2,1,0:T(8,128)(2,1)}, u32[]{:S(2)}) copy-start(bf16[2,256,256]{2,1,0:T(8,128)(2,1)} %param.26) | copy-start | bytes 786436
  74.7 126.5 %all-gather.11.cloned.1.call-start = ((), (), s32[]{:S(2)}) async-start(), calls=%async_computation.14 | async-start | bytes 2621440 | tf_op jit(solution)/shard_map/all_gather | solution.py:123
  74.7 138.6 %copy-start.39 = (f32[1,256]{1,0:T(1,128)}, f32[1,256]{1,0:T(1,128)S(1)}, u32[]{:S(2)}) copy-start(f32[1,256]{1,0:T(1,128)S(1)} %get-tuple-element.280) | copy-start | bytes 3076
  154.2 59.1 %copy-start.33 = (f32[1024]{0:T(1024)}, f32[1024]{0:T(1024)S(1)}, u32[]{:S(2)}) copy-start(f32[1024]{0:T(1024)S(1)} %get-tuple-element.274) | copy-start | bytes 12292
  156.5 58.2 %copy-start.24 = (bf16[2,256,256]{2,1,0:T(8,128)(2,1)S(1)}, bf16[2,256,256]{2,1,0:T(8,128)(2,1)}, u32[]{:S(2)}) copy-start(bf16[2,256,256]{2,1,0:T(8,128)(2,1)} %param.27) | copy-start | bytes 786436
  156.5 161.0 %reduce-scatter.11.cloned.1.call-start = ((), (), s32[]{:S(2)}) async-start(), calls=%async_computation.15 | async-start | bytes 5242880 | tf_op jit(solution)/shard_map/reduce_scatter | solution.py:126
  213.3 1.3 copy-start.10
  217.4 1.6 copy-start.1
  217.4 148.2 %all-gather.13.cloned.1.call-start = ((), (), s32[]{:S(2)}) async-start(), calls=%async_computation.16 | async-start | bytes 2621440 | tf_op jit(solution)/shard_map/all_gather | solution.py:103
  219.0 98.4 %copy-start.7 = (bf16[1024,256]{1,0:T(8,128)(2,1)S(1)}, bf16[1024,256]{1,0:T(8,128)(2,1)}, u32[]{:S(2)}) copy-start(bf16[1024,256]{1,0:T(8,128)(2,1)} %param.21) | copy-start | bytes 1572868
  320.4 1.0 copy-start.2
  322.4 150.5 %reduce-scatter.13.cloned.1.call-start = ((), (), s32[]{:S(2)}) async-start(), calls=%async_computation.17 | async-start | bytes 5242880 | tf_op jit(solution)/shard_map/reduce_scatter | solution.py:114
  376.6 15.9 %copy-start.30 = (bf16[2,64,256]{2,1,0:T(8,128)(2,1)S(1)}, bf16[2,64,256]{2,1,0:T(8,128)(2,1)}, u32[]{:S(2)}) copy-start(bf16[2,64,256]{2,1,0:T(8,128)(2,1)} %param.25) | copy-start | bytes 196612
  390.3 0.8 copy-start.23
  392.5 2.8 copy-start.16
  395.3 126.0 %all-gather.15.cloned.1.call-start = ((), (), s32[]{:S(2)}) async-start(), calls=%async_computation.18 | async-start | bytes 2621440 | tf_op jit(solution)/shard_map/all_gather | solution.py:123
  395.4 126.0 %copy-start.26 = (bf16[2,256,256]{2,1,0:T(8,128)(2,1)S(1)}, bf16[2,256,256]{2,1,0:T(8,128)(2,1)}, u32[]{:S(2)}) copy-start(bf16[2,256,256]{2,1,0:T(8,128)(2,1)} %param.26) | copy-start | bytes 786436
  474.6 1.0 copy-start.4
  476.7 91.0 %all-gather.17.cloned.1.call-start = ((), (), s32[]{:S(2)}) async-start(), calls=%async_computation.20 | async-start | bytes 2621440 | tf_op jit(solution)/shard_map/all_gather | solution.py:169
  477.4 177.8 %reduce-scatter.17.cloned.1.call-start = ((), (), s32[]{:S(2)}) async-start(), calls=%async_computation.21 | async-start | bytes 5242880 | tf_op jit(solution)/shard_map/reduce_scatter | solution.py:174
  573.6 1.3 copy-start.11
  577.7 79.4 %copy-start.8 = (bf16[1024,256]{1,0:T(8,128)(2,1)S(1)}, bf16[1024,256]{1,0:T(8,128)(2,1)}, u32[]{:S(2)}) copy-start(bf16[1024,256]{1,0:T(8,128)(2,1)} %param.21) | copy-start | bytes 1572868
  577.8 134.6 %all-gather.19.cloned.1.call-start = ((), (), s32[]{:S(2)}) async-start(), calls=%async_computation.22 | async-start | bytes 2621440 | tf_op jit(solution)/shard_map/all_gather | solution.py:184
  662.1 21.7 %all-to-all-start.2 = ((bf16[1024,4,64]{0,2,1:T(8,128)(2,1)}), bf16[1024,4,64]{0,2,1:T(8,128)(2,1)}, u32[]{:S(2)}, u32[]{:S(2)}) async-start(bf16[1024,4,64]{0,2,1:T(8,128)(2,1)} %bitcast.429), calls=%async_computation.7 | async-start | bytes 1048576 | tf_op jit(solution)/shard_map/all_to_all | solution.py:191
  666.4 196.5 %reduce-scatter.19.cloned.1.call-start = ((), (), s32[]{:S(2)}) async-start(), calls=%async_computation.23 | async-start | bytes 5242880 | tf_op jit(solution)/shard_map/reduce_scatter | solution.py:195
  756.5 2.3 copy-start.18
  756.6 2.3 copy-start.28
  761.6 179.5 %reduce-scatter.15.cloned.1.call-start = ((), (), s32[]{:S(2)}) async-start(), calls=%async_computation.19 | async-start | bytes 5242880 | tf_op jit(solution)/shard_map/reduce_scatter | solution.py:126
  765.9 225.9 %all-gather.21.cloned.1.call-start = ((), (), s32[]{:S(2)}) async-start(), calls=%async_computation.24 | async-start | bytes 2621440 | tf_op jit(solution)/shard_map/all_gather | solution.py:169
  945.3 1.0 copy-start.5
  947.2 132.3 %reduce-scatter.21.cloned.1.call-start = ((), (), s32[]{:S(2)}) async-start(), calls=%async_computation.25 | async-start | bytes 5242880 | tf_op jit(solution)/shard_map/reduce_scatter | solution.py:174
  991.8 7.4 copy-start.27
  997.8 1.4 copy-start.12
  1001.9 77.6 %copy-start.34 = (f32[1024]{0:T(1024)S(1)}, f32[1024]{0:T(1024)}, u32[]{:S(2)}) copy-start(f32[1024]{0:T(1024)} %copy-done.33) | copy-start | bytes 12292
  1001.9 77.6 %copy-start.40 = (f32[1,256]{1,0:T(1,128)S(1)}, f32[1,256]{1,0:T(1,128)}, u32[]{:S(2)}) copy-start(f32[1,256]{1,0:T(1,128)} %copy-done.39) | copy-start | bytes 3076
  1001.9 79.6 %copy-start.38 = (f32[1024]{0:T(1024)S(1)}, f32[1024]{0:T(1024)}, u32[]{:S(2)}) copy-start(f32[1024]{0:T(1024)} %get-tuple-element.273) | copy-start | bytes 12292
  1001.9 82.7 %copy-start.19 = (bf16[4,8,8,1024]{3,2,0,1:T(8,128)(2,1)S(1)}, bf16[4,8,8,1024]{3,2,0,1:T(8,128)(2,1)}, u32[]{:S(2)}) copy-start(bf16[4,8,8,1024]{3,2,0,1:T(8,128)(2,1)} %copy.85) | copy-start | bytes 1572868
  1002.0 137.1 %all-gather.23.cloned.1.call-start = ((), (), s32[]{:S(2)}) async-start(), calls=%async_computation.26 | async-start | bytes 2621440 | tf_op jit(solution)/shard_map/all_gather | solution.py:184
  1087.3 3.7 copy-start.22
  1092.1 29.9 %all-to-all-start.3 = ((bf16[1024,4,64]{0,2,1:T(8,128)(2,1)}), bf16[1024,4,64]{0,2,1:T(8,128)(2,1)}, u32[]{:S(2)}, u32[]{:S(2)}) async-start(bf16[1024,4,64]{0,2,1:T(8,128)(2,1)} %bitcast.428), calls=%async_computation.10 | async-start | bytes 1048576 | tf_op jit(solution)/shard_map/all_to_all | solution.py:191
  1096.7 7.6 copy-start.17
  1096.7 158.8 %all-reduce.5.cloned.1.call-start = ((), (), s32[]{:S(2)}) async-start(), calls=%async_computation.28 | async-start | bytes 3407872 | tf_op jit(solution)/shard_map/psum | solution.py:240
  1123.1 0.9 copy-start.20
  1123.1 5.6 copy-start.13
  1123.1 5.6 copy-start.46
  1125.0 14.0 %copy-start.31 = (bf16[2,64,256]{2,1,0:T(8,128)(2,1)S(1)}, bf16[2,64,256]{2,1,0:T(8,128)(2,1)}, u32[]{:S(2)}) copy-start(bf16[2,64,256]{2,1,0:T(8,128)(2,1)} %param.25) | copy-start | bytes 196612
  1144.7 41.8 %copy-start.15 = (bf16[4096,64]{0,1:T(8,128)(2,1)S(1)}, bf16[4096,64]{0,1:T(8,128)(2,1)}, u32[]{:S(2)}) copy-start(bf16[4096,64]{0,1:T(8,128)(2,1)} %copy-done.14) | copy-start | bytes 1572868
  1189.2 5.7 copy-start.32
  1191.9 143.0 %reduce-scatter.23.cloned.1.call-start = ((), (), s32[]{:S(2)}) async-start(), calls=%async_computation.27 | async-start | bytes 5242880 | tf_op jit(solution)/shard_map/reduce_scatter | solution.py:195
  1194.9 1.0 copy-start.21
  1198.6 136.4 %copy-start.36 = (f32[1024]{0:T(1024)S(1)}, f32[1024]{0:T(1024)}, u32[]{:S(2)}) copy-start(f32[1024]{0:T(1024)} %copy-done.35) | copy-start | bytes 12292
  1198.6 136.4 %copy-start.42 = (f32[1,256]{1,0:T(1,128)S(1)}, f32[1,256]{1,0:T(1,128)}, u32[]{:S(2)}) copy-start(f32[1,256]{1,0:T(1,128)} %copy-done.41) | copy-start | bytes 3076
  1198.6 158.8 %copy-start.3 = (f32[1024,256]{1,0:T(8,128)S(1)}, f32[1024,256]{1,0:T(8,128)}, u32[]{:S(2)}) copy-start(f32[1024,256]{1,0:T(8,128)} %reduce-scatter.9.cloned.1.call-done) | copy-start | bytes 3145732
  1198.6 158.8 %copy-start.6 = (f32[1024,256]{1,0:T(8,128)S(1)}, f32[1024,256]{1,0:T(8,128)}, u32[]{:S(2)}) copy-start(f32[1024,256]{1,0:T(8,128)} %copy-done.5) | copy-start | bytes 3145732
  1198.6 158.8 %copy-start.43 = (f32[1024]{0:T(1024)S(1)}, f32[1024]{0:T(1024)}, u32[]{:S(2)}) copy-start(f32[1024]{0:T(1024)} %get-tuple-element.271) | copy-start | bytes 12292
  (2 other events, 1.3 us)
Sparse Core Ops, SparseCore 0:
  12.0 45.2 all-gather.8
  74.8 77.3 reduce-scatter.8
  156.6 44.5 all-gather.10
  217.6 99.8 reduce-scatter.10
  322.5 43.0 all-gather.12
  395.5 77.3 reduce-scatter.12
  476.8 44.5 all-gather.14
  523.0 44.6 all-gather.16
  577.9 77.2 reduce-scatter.16
  660.1 52.1 all-gather.18
  761.7 101.1 reduce-scatter.18
  865.2 75.8 reduce-scatter.14
  947.3 44.5 all-gather.20
  1002.1 77.3 reduce-scatter.20
  1084.8 54.1 all-gather.22
  1192.1 63.4 all-reduce.4
  1257.8 77.1 reduce-scatter.22
where the time goes:
time: 1390 us; the launch traced here: 1370 us
  waiting for transfers between devices  903 us (65%)
  blocking collectives  135 us (10%)
  matrix products  132 us (9%)
  local copies, waits for them, and re-layouts  119 us (9%)
  other arithmetic  52.4 us (4%)
  between operations  15 us (1%)
    reduce_scatter x2, waiting for transfers between devices, forward_layer(): lax.psum_scatter(jnp.dot(attn_mix, w_out_l, preferred_element_type=jnp.fl...  155 us
    reduce_scatter x2, waiting for transfers between devices, backward_layer(): lax.psum_scatter(jnp.einsum('rf,df->rd', grad_pre, w_up_l, preferred_elem...  155 us
    all_to_all x2, blocking collectives, forward_layer(): lax.all_to_all(cross_cols, 'head', split_axis=0, concat_axis=1, tiled=True)  115 us
    reduce_scatter x2, waiting for transfers between devices, forward_layer(): lax.psum_scatter(jnp.dot(hidden, w_down_l, preferred_element_type=jnp.flo...  114 us
    reduce_scatter x2, waiting for transfers between devices, backward_layer(): lax.psum_scatter(from_qkv + jnp.einsum('rc,dc->rd', cross_cols, w_cross_l...  105 us
    all_gather x2, waiting for transfers between devices, forward_layer(): gathered_two = lax.all_gather(normed_two, 'head', axis=0, tiled=True)  88.5 us
    all_gather x2, waiting for transfers between devices, forward_layer(): gathered = lax.all_gather(normed, 'head', axis=0, tiled=True)  86.7 us
    all_gather x2, waiting for transfers between devices, backward_layer(): feed_rows = lax.all_gather(grad_feed, 'head', axis=0, tiled=True)  78.6 us
  transfers between devices with their start and end apart: 19, of which 19 were waited for; matrix products, arithmetic and copies ran while one was open for 6% of the time, Pallas kernels for 0%

commit v1 on v0

v1 whole, which is shorter than its diff:
```python
import functools

import jax
import jax.numpy as jnp
from jax import lax
from jax.experimental import pallas as pl
from jax.experimental.pallas import tpu as pltpu
from jax.sharding import PartitionSpec as P

HD = 64
LAYERS = 2
EPSILON = 1e-06
MASKED_SCORE = -1000000000.0
BF = jnp.bfloat16
F32 = jnp.float32

VMEM_LIMIT = 48 * 2**20


def nn(a, b):
    return lax.dot_general(a, b, (((1,), (0,)), ((), ())), preferred_element_type=F32)


def nt(a, b):
    return lax.dot_general(a, b, (((1,), (1,)), ((), ())), preferred_element_type=F32)


def tn(a, b):
    return lax.dot_general(a, b, (((0,), (0,)), ((), ())), preferred_element_type=F32)


def rescale_of(values):
    return lax.rsqrt(jnp.mean(values * values, axis=-1, keepdims=True) + EPSILON)


def norm_back(values, rescale, gain, gradient):
    scaled = gradient * gain
    product_mean = jnp.mean(values * scaled, axis=-1, keepdims=True)
    normal = values * rescale
    grad_values = rescale * (scaled - normal * (rescale * product_mean))
    return grad_values, jnp.sum(gradient * normal, axis=0, keepdims=True)


def gelu_and_slope(u):
    t = 1.0 / (1.0 + (0.3275911 * 0.7071067811865476) * jnp.abs(u))
    e = jnp.exp(-0.5 * (u * u))
    poly = ((((0.5 * 1.061405429) * t - 0.5 * 1.453152027) * t + 0.5 * 1.421413741) * t - 0.5 * 0.284496736) * t + 0.5 * 0.254829592
    tail = poly * t * e
    cdf = jnp.where(u >= 0.0, 1.0 - tail, tail)
    return u * cdf, cdf + u * (e * 0.3989422804014327)


def load_pieces(own, mine, theirs, dst, half_at, sem):
    half = dst.shape[1] // 2
    keep = pl.multiple_of(half_at * half, 16)
    other = pl.multiple_of((1 - half_at) * half, 16)
    copies = [pltpu.make_async_copy(own, dst.at[0], sem)]
    for m, ref in enumerate(mine):
        copies.append(pltpu.make_async_copy(ref, dst.at[m + 1, pl.ds(keep, half)], sem))
    for m, ref in enumerate(theirs):
        copies.append(pltpu.make_async_copy(ref, dst.at[m + 1, pl.ds(other, half)], sem))
    for copy in copies:
        copy.start()
    for copy in copies:
        copy.wait()


def spread_attn(wa, w_cross, w_out, bias, head_at, heads):
    total = jnp.zeros((1, 256), F32)
    for m in range(heads):
        place = pl.multiple_of((head_at ^ m) * HD, HD)
        w_cross[pl.ds(place, HD), :] = wa[m, 192:256, :]
        w_out[m * HD:(m + 1) * HD, :] = wa[m, 256:320, :]
        total = total + wa[m, 320:336, :].astype(F32)[0:1, :]
    bias[...] = jnp.broadcast_to(total, bias.shape)


def attn_fwd_kernel(info, lens, cur_ref, gain_ref, own, m1, m2, m3, t1, t2, t3,
                    middle_ref, base_ref, nrm_ref, qkv_ref, mix_ref, lse_ref,
                    wa, w_cross, w_out, bias, sem):
    step = pl.program_id(0)

    @pl.when(step == 0)
    def _():
        load_pieces(own, (m1, m2, m3), (t1, t2, t3), wa, info[1], sem)
        spread_attn(wa, w_cross, w_out, bias, info[0], 4)

    length = lens[info[2] + step]
    cur = cur_ref[...].astype(F32)
    nrm = (cur * rescale_of(cur) * gain_ref[...]).astype(BF)
    nrm_ref[...] = nrm
    slots = lax.broadcasted_iota(jnp.int32, (256, 256), 0)
    valid = slots < length
    for m in range(4):
        qkv = nt(wa[m, 0:192, :], nrm).astype(BF)
        qkv_ref[m * 192:(m + 1) * 192, :] = qkv
        scores = tn(qkv[64:128], qkv[0:64] * BF(0.125))
        scores = jnp.where(valid, scores, MASKED_SCORE)
        top = jnp.max(scores, axis=0, keepdims=True)
        e = jnp.exp(scores - top)
        total = jnp.sum(e, axis=0, keepdims=True)
        p = (e * (1.0 / total)).astype(BF)
        mix_ref[m * HD:(m + 1) * HD, :] = nn(qkv[128:192], p).astype(BF)
        lse_ref[m:m + 1, :] = top + jnp.log(total)
    middle = cur + tn(mix_ref[...], w_out[...])
    middle_ref[...] = middle
    cross = nt(nrm, w_cross[...]) + bias[0:1, :]
    base_ref[...] = middle + cur * cross


def mlp_fwd_block(middle, gain, wm):
    r = rescale_of(middle)
    n2 = (middle * r * gain).astype(BF)
    feed = None
    kept = []
    for m in range(4):
        u = nn(n2, wm[m, 0:256, :])
        hid, slope = gelu_and_slope(u)
        hid = hid.astype(BF)
        kept.append((hid, slope.astype(BF)))
        part = nn(hid, wm[m, 256:512, :])
        feed = part if feed is None else feed + part
    return r, n2, kept, feed


def mlp_fwd_kernel(info, middle_ref, base_ref, gain_ref, own, m1, m2, m3, t1, t2, t3,
                   out_ref, hid_ref, slope_ref, wm, sem):
    @pl.when(pl.program_id(0) == 0)
    def _():
        load_pieces(own, (m1, m2, m3), (t1, t2, t3), wm, info[1], sem)

    _, _, kept, feed = mlp_fwd_block(middle_ref[...], gain_ref[...], wm)
    for m, (hid, slope) in enumerate(kept):
        hid_ref[:, m * 256:(m + 1) * 256] = hid
        slope_ref[:, m * 256:(m + 1) * 256] = slope
    out_ref[...] = base_ref[...] + feed


def mlp_bwd_block(grad, middle, r, n2, kept, gain, wm, acc, small):
    gf = grad.astype(BF)
    gn = None
    for m in range(4):
        hid, slope = kept[m]
        gp = (nt(gf, wm[m, 256:512, :]) * slope.astype(F32)).astype(BF)
        acc[1, m] += tn(hid, gf)
        acc[0, m] += tn(n2, gp)
        part = nt(gp, wm[m, 0:256, :])
        gn = part if gn is None else gn + part
    back, gain_grad = norm_back(middle, r, gain, gn)
    small[0:1, :] += gain_grad
    return grad + back


def emit_mlp_grads(info, acc, keep_ref, send_ref):
    keep_ref[...] = acc[info[1]].astype(BF)
    send_ref[...] = acc[1 - info[1]].astype(BF)


def mlp_both_kernel(info, middle_ref, base_ref, cot_ref, gain_ref, own, m1, m2, m3, t1, t2, t3,
                    out_ref, gm_ref, keep_ref, send_ref, small_ref, wm, acc, sem):
    step = pl.program_id(0)

    @pl.when(step == 0)
    def _():
        load_pieces(own, (m1, m2, m3), (t1, t2, t3), wm, info[1], sem)
        acc[...] = jnp.zeros_like(acc)
        small_ref[...] = jnp.zeros_like(small_ref)

    middle = middle_ref[...]
    gain = gain_ref[...]
    r, n2, kept, feed = mlp_fwd_block(middle, gain, wm)
    out_ref[...] = base_ref[...] + feed
    grad = cot_ref[...].astype(F32)
    gm_ref[...] = mlp_bwd_block(grad, middle, r, n2, kept, gain, wm, acc, small_ref)

    @pl.when(step == pl.num_programs(0) - 1)
    def _():
        emit_mlp_grads(info, acc, keep_ref, send_ref)


def mlp_bwd_kernel(info, grad_ref, middle_ref, hid_ref, slope_ref, gain_ref, own, m1, m2, m3, t1, t2, t3,
                   gm_ref, keep_ref, send_ref, small_ref, wm, acc, sem):
    step = pl.program_id(0)

    @pl.when(step == 0)
    def _():
        load_pieces(own, (m1, m2, m3), (t1, t2, t3), wm, info[1], sem)
        acc[...] = jnp.zeros_like(acc)
        small_ref[...] = jnp.zeros_like(small_ref)

    middle = middle_ref[...]
    gain = gain_ref[...]
    r = rescale_of(middle)
    n2 = (middle * r * gain).astype(BF)
    kept = [(hid_ref[:, m * 256:(m + 1) * 256], slope_ref[:, m * 256:(m + 1) * 256]) for m in range(4)]
    gm_ref[...] = mlp_bwd_block(grad_ref[...], middle, r, n2, kept, gain, wm, acc, small_ref)

    @pl.when(step == pl.num_programs(0) - 1)
    def _():
        emit_mlp_grads(info, acc, keep_ref, send_ref)


def attn_bwd_kernel(info, lens, grad_ref, gm_ref, cur_ref, nrm_ref, qkv_ref, mix_ref, lse_ref, gain_ref,
                    own, m1, m2, m3, t1, t2, t3,
                    out_ref, keep_ref, send_ref, small_ref,
                    wa, w_cross, w_out, bias, d_qkv, d_cross, d_out, payload, sem):
    step = pl.program_id(0)

    @pl.when(step == 0)
    def _():
        load_pieces(own, (m1, m2, m3), (t1, t2, t3), wa, info[1], sem)
        spread_attn(wa, w_cross, w_out, bias, info[0], 4)
        d_qkv[...] = jnp.zeros_like(d_qkv)
        d_cross[...] = jnp.zeros_like(d_cross)
        d_out[...] = jnp.zeros_like(d_out)
        small_ref[...] = jnp.zeros_like(small_ref)

    length = lens[info[2] + step]
    valid = lax.broadcasted_iota(jnp.int32, (256, 256), 0) < length
    grad = grad_ref[...].astype(F32)
    gm = gm_ref[...]
    cur = cur_ref[...].astype(F32)
    nrm = nrm_ref[...]
    ga = gm.astype(BF)
    d_out[...] += nn(mix_ref[...], ga)
    gmix = nt(w_out[...], ga).astype(BF)
    gc = (grad * cur).astype(BF)
    d_cross[...] += tn(gc, nrm)
    gn = nn(gc, w_cross[...])
    cross = nt(nrm, w_cross[...]) + bias[0:1, :]
    for m in range(4):
        q = qkv_ref[m * 192:m * 192 + 64, :]
        k = qkv_ref[m * 192 + 64:m * 192 + 128, :]
        v = qkv_ref[m * 192 + 128:m * 192 + 192, :]
        go = gmix[m * HD:(m + 1) * HD]
        scores = tn(k, q * BF(0.125))
        scores = jnp.where(valid, scores, MASKED_SCORE)
        p = jnp.exp(scores - lse_ref[m:m + 1, :])
        gv = nt(go, p.astype(BF))
        gp = tn(v, go)
        dot = jnp.sum(gp * p, axis=0, keepdims=True)
        gs = (p * (gp - dot)).astype(BF)
        gq = nn(k, gs) * 0.125
        gk = nt(q, gs) * 0.125
        gqkv = jnp.concatenate([gq, gk, gv], axis=0).astype(BF)
        d_qkv[m * 192:(m + 1) * 192, :] += nn(gqkv, nrm)
        gn = gn + tn(gqkv, wa[m, 0:192, :])
    r = rescale_of(cur)
    back, gain_grad = norm_back(cur, r, gain_ref[...], gn)
    small_ref[0:1, :] += gain_grad
    small_ref[1:2, :] += jnp.sum(gc.astype(F32), axis=0, keepdims=True)
    out_ref[...] = gm + grad * cross + back

    @pl.when(step == pl.num_programs(0) - 1)
    def _():
        for m in range(4):
            place = pl.multiple_of((info[0] ^ m) * HD, HD)
            payload[m, 0:192, :] = d_qkv[m * 192:(m + 1) * 192, :].astype(BF)
            payload[m, 192:256, :] = d_cross[pl.ds(place, HD), :].astype(BF)
            payload[m, 256:320, :] = d_out[m * HD:(m + 1) * HD, :].astype(BF)
        keep = pl.multiple_of(info[1] * 160, 16)
        other = pl.multiple_of((1 - info[1]) * 160, 16)
        for m in range(4):
            keep_ref[m] = payload[m, pl.ds(keep, 160), :]
            send_ref[m] = payload[m, pl.ds(other, 160), :]


SMEM = pl.BlockSpec(memory_space=pltpu.SMEM)
ANY = pl.BlockSpec(memory_space=pl.ANY)


def row_spec(width):
    return pl.BlockSpec((256, width), lambda s: (s, 0))


def col_spec(height):
    return pl.BlockSpec((height, 256), lambda s: (0, s))


def whole(shape):
    return pl.BlockSpec(shape, lambda s: (0,) * len(shape))


def call(kernel, rows, in_specs, outs, scratch, flops, name):
    shapes = [jax.ShapeDtypeStruct(shape, dtype) for shape, dtype, _ in outs]
    return pl.pallas_call(
        kernel,
        grid=(rows // 256,),
        in_specs=in_specs,
        out_specs=[spec for _, _, spec in outs],
        out_shape=shapes,
        scratch_shapes=scratch,
        compiler_params=pltpu.CompilerParams(vmem_limit_bytes=VMEM_LIMIT, dimension_semantics=("arbitrary",)),
        cost_estimate=pl.CostEstimate(flops=flops, bytes_accessed=8 * 2**20, transcendentals=2 * 2**20),
        name=name,
    )


ATTN_SCRATCH = [
    pltpu.VMEM((4, 352, 256), BF),
    pltpu.VMEM((256, 256), BF),
    pltpu.VMEM((256, 256), BF),
    pltpu.VMEM((8, 256), F32),
]


def attn_fwd(info, lens, cur, gain, pieces):
    rows = cur.shape[0]
    outs = [
        ((rows, 256), F32, row_spec(256)),
        ((rows, 256), F32, row_spec(256)),
        ((rows, 256), BF, row_spec(256)),
        ((768, rows), BF, col_spec(768)),
        ((256, rows), BF, col_spec(256)),
        ((8, rows), F32, col_spec(8)),
    ]
    return call(
        attn_fwd_kernel, rows, [SMEM, SMEM, row_spec(256), whole((1, 256))] + [ANY] * 7, outs,
        ATTN_SCRATCH + [pltpu.SemaphoreType.DMA], 2 * 10**9, "attn_fwd",
    )(info, lens, cur, gain, *pieces)


def mlp_fwd(info, middle, base, gain, pieces):
    rows = middle.shape[0]
    outs = [
        ((rows, 256), F32, row_spec(256)),
        ((rows, 1024), BF, row_spec(1024)),
        ((rows, 1024), BF, row_spec(1024)),
    ]
    return call(
        mlp_fwd_kernel, rows, [SMEM, row_spec(256), row_spec(256), whole((1, 256))] + [ANY] * 7, outs,
        [pltpu.VMEM((4, 512, 256), BF), pltpu.SemaphoreType.DMA], 2 * 10**9, "mlp_fwd",
    )(info, middle, base, gain, *pieces)


MLP_GRADS = [
    ((4, 256, 256), BF, whole((4, 256, 256))),
    ((4, 256, 256), BF, whole((4, 256, 256))),
    ((8, 256), F32, whole((8, 256))),
]
MLP_SCRATCH = [
    pltpu.VMEM((4, 512, 256), BF),
    pltpu.VMEM((2, 4, 256, 256), F32),
    pltpu.SemaphoreType.DMA,
]


def mlp_both(info, middle, base, cot, gain, pieces):
    rows = middle.shape[0]
    outs = [((rows, 256), F32, row_spec(256)), ((rows, 256), F32, row_spec(256))] + MLP_GRADS
    return call(
        mlp_both_kernel, rows, [SMEM] + [row_spec(256)] * 3 + [whole((1, 256))] + [ANY] * 7, outs,
        MLP_SCRATCH, 4 * 10**9, "mlp_both",
    )(info, middle, base, cot, gain, *pieces)


def mlp_bwd(info, grad, middle, hid, slope, gain, pieces):
    rows = middle.shape[0]
    outs = [((rows, 256), F32, row_spec(256))] + MLP_GRADS
    return call(
        mlp_bwd_kernel, rows,
        [SMEM, row_spec(256), row_spec(256), row_spec(1024), row_spec(1024), whole((1, 256))] + [ANY] * 7, outs,
        MLP_SCRATCH, 4 * 10**9, "mlp_bwd",
    )(info, grad, middle, hid, slope, gain, *pieces)


def attn_bwd(info, lens, grad, gm, cur, saved, gain, pieces):
    nrm, qkv, mix, lse = saved
    rows = cur.shape[0]
    outs = [
        ((rows, 256), F32, row_spec(256)),
        ((4, 160, 256), BF, whole((4, 160, 256))),
        ((4, 160, 256), BF, whole((4, 160, 256))),
        ((8, 256), F32, whole((8, 256))),
    ]
    scratch = ATTN_SCRATCH + [
        pltpu.VMEM((768, 256), F32),
        pltpu.VMEM((256, 256), F32),
        pltpu.VMEM((256, 256), F32),
        pltpu.VMEM((4, 320, 256), BF),
        pltpu.SemaphoreType.DMA,
    ]
    return call(
        attn_bwd_kernel, rows,
        [SMEM, SMEM] + [row_spec(256)] * 4 + [col_spec(768), col_spec(256), col_spec(8), whole((1, 256))] + [ANY] * 7, outs,
        scratch, 4 * 10**9, "attn_bwd",
    )(info, lens, grad, gm, cur, nrm, qkv, mix, lse, gain, *pieces)


def swap(x, axis, size, mask):
    return lax.ppermute(x, axis, [(i, i ^ mask) for i in range(size)])


def gather_pieces(own, half_at, head_size, dp_size):
    half = own.shape[0] // 2
    part = lax.dynamic_slice_in_dim(own, half_at * half, half, 0)
    mine = [swap(part, "head", head_size, m) for m in range(1, head_size)]
    theirs = [swap(x, "dp", dp_size, 1) for x in mine]
    return [own] + mine + theirs


def add(*terms):
    total = terms[0].astype(F32)
    for term in terms[1:]:
        total = total + term.astype(F32)
    return total


def sum_over_rest(x, dp_size, dtype):
    bit = 2
    while bit < dp_size:
        if bit * 2 < dp_size:
            a, b, c = (swap(x, "dp", dp_size, mask) for mask in (bit, 2 * bit, 3 * bit))
            x = add(x, a) + add(b, c)
            bit *= 4
        else:
            x = add(x, swap(x, "dp", dp_size, bit))
            bit *= 2
        x = x.astype(dtype)
    return x


def reduce_pieces(keep, send, half_at, head_size, dp_size):
    got = swap(send, "dp", dp_size, 1)
    sums = [add(keep[m], got[m]).astype(BF) for m in range(head_size)]
    a, b, c = (swap(sums[m], "head", head_size, m) for m in range(1, head_size))
    mine = (add(sums[0], a) + add(b, c)).astype(BF)
    mine = sum_over_rest(mine, dp_size, BF)
    theirs = swap(mine, "dp", dp_size, 1)
    first = half_at == 0
    return jnp.where(first, mine, theirs).astype(F32), jnp.where(first, theirs, mine).astype(F32)


def sum_all(x, head_size, dp_size):
    x = add(x, swap(x, "dp", dp_size, 1))
    a, b, c = (swap(x, "head", head_size, m) for m in range(1, head_size))
    x = add(x, a) + add(b, c)
    return sum_over_rest(x, dp_size, F32)


def solution(mesh):
    dp_size, head_size = mesh.shape["dp"], mesh.shape["head"]
    reduce_group = functools.partial(reduce_pieces, head_size=head_size, dp_size=dp_size)

    def body(tokens, lengths, cotangent, gain_attn, gain_mlp, w_qkv, w_out, w_up, w_down, w_cross, b_cross):
        head_at = lax.axis_index("head")
        half_at = lax.axis_index("dp") % 2
        samples = tokens.shape[0] // 256
        info = jnp.stack([head_at, half_at, head_at * samples]).astype(jnp.int32)
        width = b_cross.shape[1]
        attn_w, mlp_w = [], []
        for l in range(LAYERS):
            bias = lax.dynamic_update_slice(jnp.zeros((32, 256), BF), b_cross[l][None, :], (0, head_at * width))
            own = jnp.concatenate([
                w_qkv[l].transpose(1, 2, 0).reshape(3 * HD, 256), w_cross[l].T, w_out[l], bias])
            attn_w.append(gather_pieces(own, half_at, head_size, dp_size))
            own = jnp.concatenate([w_up[l], w_down[l]])
            mlp_w.append(gather_pieces(own, half_at, head_size, dp_size))
        ga = [gain_attn[l][None, :] for l in range(LAYERS)]
        gf = [gain_mlp[l][None, :] for l in range(LAYERS)]

        mid0, base0, *saved0 = attn_fwd(info, lengths, tokens, ga[0], attn_w[0])
        cur1, hid0, slope0 = mlp_fwd(info, mid0, base0, gf[0], mlp_w[0])
        mid1, base1, *saved1 = attn_fwd(info, lengths, cur1, ga[1], attn_w[1])
        output, gm1, keep_m1, send_m1, small_m1 = mlp_both(info, mid1, base1, cotangent, gf[1], mlp_w[1])
        grad1, keep_a1, send_a1, small_a1 = attn_bwd(info, lengths, cotangent, gm1, cur1, saved1, ga[1], attn_w[1])
        gm0, keep_m0, send_m0, small_m0 = mlp_bwd(info, grad1, mid0, hid0, slope0, gf[0], mlp_w[0])
        grad0, keep_a0, send_a0, small_a0 = attn_bwd(info, lengths, grad1, gm0, tokens, saved0, ga[0], attn_w[0])

        m1 = reduce_group(keep_m1, send_m1, half_at)
        a1 = reduce_group(keep_a1, send_a1, half_at)
        m0 = reduce_group(keep_m0, send_m0, half_at)
        a0 = reduce_group(keep_a0, send_a0, half_at)
        small = sum_all(
            jnp.concatenate([small_a0[0:2], small_m0[0:1], small_a1[0:2], small_m1[0:1], jnp.zeros((2, 256), F32)]),
            head_size, dp_size)
        attn = [jnp.concatenate(a) for a in (a0, a1)]
        d_qkv = jnp.stack([a[0:192].reshape(3, HD, 256).transpose(2, 0, 1) for a in attn])
        d_cross = jnp.stack([a[192:256].T for a in attn])
        d_out = jnp.stack([a[256:320] for a in attn])
        d_up = jnp.stack([m0[0], m1[0]])
        d_down = jnp.stack([m0[1], m1[1]])
        d_bias = lax.dynamic_slice(small[1:5:3], (0, head_at * width), (LAYERS, width))
        return (output, grad0, small[0:4:3], small[2:6:3], d_qkv, d_out, d_up, d_down, d_cross, d_bias)

    rows, weights = P(("dp", "head"), None), P(None, "head", None)
    return jax.shard_map(
        body,
        mesh=mesh,
        in_specs=(rows, P("dp"), rows, P(), P(), P(None, None, None, "head"), weights, P(None, None, "head"),
                  weights, P(None, None, "head"), P(None, "head")),
        out_specs=(rows, rows, P(), P(), P(None, None, None, "head"), weights, P(None, None, "head"),
                   weights, P(None, None, "head"), P(None, "head")),
        check_vma=False,
    )
```

time: 1390 us -> 208 us (0.15); the launches traced: 1370 us -> 207 us
  waiting for transfers between devices: 903 us -> 38.6 us
  blocking collectives: 135 us -> 0 us
  matrix products: 132 us -> 0 us
  local copies, waits for them, and re-layouts: 119 us -> 9.65 us
  Pallas kernels: 0 us -> 73.8 us
  starting transfers between devices: 9.98 us -> 72.9 us
  other arithmetic: 52.4 us -> 11.1 us
    reduce_scatter x8 -> x0, waiting for transfers between devices: 529 us -> none  [the longest x2 155 us: forward_layer(): lax.psum_scatter(jnp.dot(attn_mix, w_out_l, preferred_element_type=jnp.fl...]
    all_gather x8 -> x0, waiting for transfers between devices: 289 us -> none  [the longest x2 88.5 us: forward_layer(): gathered_two = lax.all_gather(normed_two, 'head', axis=0, tiled=True)]
    dot_general x138 -> x0, matrix products: 121 us -> none  [the longest x2 24.5 us: forward_layer(): pre_act = jnp.dot(gathered_two, w_up_l, preferred_element_type=jnp.float32)]
    all_to_all x2 -> x0, blocking collectives: 115 us -> none  [forward_layer(): lax.all_to_all(cross_cols, 'head', split_axis=0, concat_axis=1, tiled=True)]
    pallas_call x0 -> x7, Pallas kernels: none -> 73.8 us  [the longest x2 28.8 us: attn_bwd(): call(attn_bwd_kernel, rows, [SMEM, SMEM] + [row_spec(256)] * 4 + [col_spe...]
    ppermute x0 -> x63, starting transfers between devices: none -> 72.9 us  [swap(): return lax.ppermute(x, axis, [(i, i ^ mask) for i in range(size)])]
    psum x1 -> x0, waiting for transfers between devices: 54.2 us -> none  [body(): lax.psum((grad_qkv_w, grad_out, grad_up, grad_down, grad_cross_w, grad_bi...]
    ppermute x0 -> x63, waiting for transfers between devices: none -> 38.6 us  [swap(): return lax.ppermute(x, axis, [(i, i ^ mask) for i in range(size)])]
  transfers between devices with their start and end apart: 19 -> 63, of which waited for: 19 -> 18; matrix products, arithmetic and copies ran while one was open for 6% -> 6% of each run, Pallas kernels for 0% -> 13%
where the time goes in v1:
time: 208 us; the launch traced here: 207 us
  Pallas kernels  73.8 us (35%)
  starting transfers between devices  72.9 us (35%)
  waiting for transfers between devices  38.6 us (19%)
  other arithmetic  11.1 us (5%)
  local copies, waits for them, and re-layouts  9.65 us (5%)
    ppermute x63, starting transfers between devices, swap(): return lax.ppermute(x, axis, [(i, i ^ mask) for i in range(size)])  72.9 us
    ppermute x63, waiting for transfers between devices, swap(): return lax.ppermute(x, axis, [(i, i ^ mask) for i in range(size)])  38.6 us
    pallas_call x2, Pallas kernels, attn_bwd(): call(attn_bwd_kernel, rows, [SMEM, SMEM] + [row_spec(256)] * 4 + [col_spe...  28.8 us
    pallas_call x2, Pallas kernels, attn_fwd(): call(attn_fwd_kernel, rows, [SMEM, SMEM, row_spec(256), whole((1, 256))]...  19.7 us
    pallas_call x1, Pallas kernels, mlp_both(): call(mlp_both_kernel, rows, [SMEM] + [row_spec(256)] * 3 + [whole((1, 256...  10.4 us
    pallas_call x1, Pallas kernels, mlp_fwd(): call(mlp_fwd_kernel, rows, [SMEM, row_spec(256), row_spec(256), whole((1,...  7.71 us
    pallas_call x1, Pallas kernels, mlp_bwd(): call(mlp_bwd_kernel, rows, [SMEM, row_spec(256), row_spec(256), row_spec(...  7.28 us
  transfers between devices with their start and end apart: 63, of which 18 were waited for; matrix products, arithmetic and copies ran while one was open for 6% of the time, Pallas kernels for 13%

profile of v1, /device:TPU:9, one launch (start us, length us, event | category | flops | bytes accessed | tf_op | source)
XLA Modules:
  0.0 207.4 jit_solution(7648350349892849788)
XLA Ops:
  1.4 1.0 fusion.26
  2.4 0.8 slice_bitcast_fusion.9
  3.2 0.8 slice_bitcast_fusion.8
  4.4 2.4 %collective-permute-start.1 = (bf16[176,256]{1,0:T(8,128)(2,1)S(1)}, bf16[176,256]{1,0:T(8,128)(2,1)S(1)}, u32[]{:S(2)}, u32[]{:S(2)}) collective-permute-start(bf16[176,256]{1,0:T(8,128)(2,1)S(1)} %constant_dynamic-slice_fusion.2), channel_id=1, source_target_pairs={{0,2},{1,3},{2,0},{3,1},{4,6},{5,7},{6,4},{7,5},{8,10},{9,11},{10,... | collective-permute-start | bytes 270344 | tf_op jit(solution)/shard_map/ppermute | solution.py:391
  7.1 1.1 slice_bitcast_fusion
  8.5 3.3 %collective-permute-start.7 = (bf16[256,256]{1,0:T(8,128)(2,1)S(1)}, bf16[256,256]{1,0:T(8,128)(2,1)S(1)}, u32[]{:S(2)}, u32[]{:S(2)}) collective-permute-start(bf16[256,256]{1,0:T(8,128)(2,1)S(1)} %fusion.17), channel_id=1, source_target_pairs={{0,2},{1,3},{2,0},{3,1},{4,6},{5,7},{6,4},{7,5},{8,10},{9,11},{10,... | collective-permute-start | bytes 393224 | tf_op jit(solution)/shard_map/ppermute | solution.py:391
  12.2 1.2 collective-permute-start.6
  13.8 6.8 %collective-permute-done.2.m3 = bf16[176,256]{1,0:T(8,128)(2,1)S(1)} collective-permute-done((bf16[176,256]{1,0:T(8,128)(2,1)S(1)}, bf16[176,256]{1,0:T(8,128)(2,1)S(1)}, u32[]{:S(2)}, u32[]{:S(2)}) %collective-permute-start.2) | collective-permute-done | bytes 90144 | tf_op jit(solution)/shard_map/ppermute | solution.py:391
  20.9 1.7 collective-permute-done.12.m1
  22.6 3.2 %collective-permute-start.3 = (bf16[176,256]{1,0:T(8,128)(2,1)S(1)}, bf16[176,256]{1,0:T(8,128)(2,1)S(1)}, u32[]{:S(2)}, u32[]{:S(2)}) collective-permute-start(bf16[176,256]{1,0:T(8,128)(2,1)S(1)} %collective-permute-done.m1), channel_id=1, source_target_pairs={{0,4},{4,0},{8,12},{12,8},{16,20},{20,16},{24,28},{28,24},{1,5},{5... | collective-permute-start | bytes 270344 | tf_op jit(solution)/shard_map/ppermute | solution.py:391
  25.7 3.1 %collective-permute-done.13.m2 = bf16[176,256]{1,0:T(8,128)(2,1)S(1)} collective-permute-done((bf16[176,256]{1,0:T(8,128)(2,1)S(1)}, bf16[176,256]{1,0:T(8,128)(2,1)S(1)}, u32[]{:S(2)}, u32[]{:S(2)}) %collective-permute-start.13) | collective-permute-done | bytes 90144 | tf_op jit(solution)/shard_map/ppermute | solution.py:391
  28.9 1.7 collective-permute-start.4
  31.0 4.0 %collective-permute-start.18 = (bf16[256,256]{1,0:T(8,128)(2,1)S(1)}, bf16[256,256]{1,0:T(8,128)(2,1)S(1)}, u32[]{:S(2)}, u32[]{:S(2)}) collective-permute-start(bf16[256,256]{1,0:T(8,128)(2,1)S(1)} %fusion.16), channel_id=1, source_target_pairs={{0,1},{1,0},{2,3},{3,2},{4,5},{5,4},{6,7},{7,6},{8,9},{9,8},{10,11... | collective-permute-start | bytes 393224 | tf_op jit(solution)/shard_map/ppermute | solution.py:391
  35.0 1.0 collective-permute-start.10
  36.5 9.8 %attn_fwd.2 = (f32[1024,256]{1,0:T(8,128)S(1)}, f32[1024,256]{1,0:T(8,128)S(1)}, bf16[1024,256]{1,0:T(8,128)(2,1)S(1)}, bf16[768,1024]{1,0:T(8,128)(2,1)S(1)}, b...) custom-call(s32[3]{0:T(128)S(1)} %pad_add_fusion.info, s32[16]{0:T(128)S(1)} %copy-done.14, ...), custom_call_target="tpu_custom_call" | custom-call | flops 2000000000 | bytes 8388608 | tf_op jit(solution)/shard_map/attn_fwd/pallas_call | solution.py:317
  46.3 1.2 copy-done.15
  47.5 1.0 collective-permute-start.20
  49.6 7.7 %mlp_fwd.1 = (f32[1024,256]{1,0:T(8,128)S(1)}, bf16[1024,1024]{1,0:T(8,128)(2,1)}, bf16[1024,1024]{1,0:T(8,128)(2,1)}) custom-call(s32[3]{0:T(128)S(1)} %pad_add_fusion.info, f32[1024,256]{1,0:T(8,128)S(1)} %get-tuple-element.42.middle_ref, f32[1024,256]{1,0:T(8,128)S(1)} %get-tuple-element.43.base_ref, f32[1,256]{1,0:T(1,128)S(1)} %get-tuple-element.109.gain_ref, ...), custom_call_target="tpu_custom_call" | custom-call | flops 2000000000 | bytes 8388608 | tf_op jit(solution)/shard_map/mlp_fwd/pallas_call | solution.py:330
  57.5 3.0 %collective-permute-done.20.m3 = bf16[256,256]{1,0:T(8,128)(2,1)S(1)} collective-permute-done((bf16[256,256]{1,0:T(8,128)(2,1)S(1)}, bf16[256,256]{1,0:T(8,128)(2,1)S(1)}, u32[]{:S(2)}, u32[]{:S(2)}) %collective-permute-start.20) | collective-permute-done | bytes 131104 | tf_op jit(solution)/shard_map/ppermute | solution.py:391
  60.5 0.9 collective-permute-start.22
  61.4 10.0 %attn_fwd.3 = (f32[1024,256]{1,0:T(8,128)S(1)}, f32[1024,256]{1,0:T(8,128)S(1)}, bf16[1024,256]{1,0:T(8,128)(2,1)S(1)}, bf16[768,1024]{1,0:T(8,128)(2,1)}, bf16[...) custom-call(s32[3]{0:T(128)S(1)} %pad_add_fusion.info, s32[16]{0:T(128)S(1)} %copy-done.14, ...), custom_call_target="tpu_custom_call" | custom-call | flops 2000000000 | bytes 8388608 | tf_op jit(solution)/shard_map/attn_fwd/pallas_call | solution.py:317
  71.4 10.4 %mlp_both.1 = (f32[1024,256]{1,0:T(8,128)}, f32[1024,256]{1,0:T(8,128)S(1)}, bf16[4,256,256]{2,1,0:T(8,128)(2,1)S(1)}, bf16[4,256,256]{2,1,0:T(8,128)(2,1)S(1)}, f32[8,256]{1,0:T(8,128)S(1)}) custom-call(s32[3]{0:T(128)S(1)} %pad_add_fusion.info, f32[1024,256]{1,0:T(8,128)S(1)} %get-tuple-element.45.middle_ref, f32[1024,256]{1,0:T(8,128)S(1)} %get-tuple-element.46.base_ref, ...), custom_call_target="tpu_custom_call" | custom-call | flops 4000000000 | bytes 8388608 | tf_op jit(solution)/shard_map/mlp_both/pallas_call | solution.py:351
  81.8 14.1 %attn_bwd.2 = (f32[1024,256]{1,0:T(8,128)S(1)}, bf16[4,160,256]{2,1,0:T(8,128)(2,1)S(1)}, bf16[4,160,256]{2,1,0:T(8,128)(2,1)S(1)}, f32[8,256]{1,0:T(8,128)S(1)}) custom-call(s32[3]{0:T(128)S(1)} %pad_add_fusion.info, s32[16]{0:T(128)S(1)} %copy-done.14, bf16[1024,256]{1,0:T(8,128)(2,1)S(1)} %copy-done, f32[1024,256]{1,0:T(8,128)S(1)} %get-tuple-element.48.gm_ref, ...), custom_call_target="tpu_custom_call" | custom-call | flops 4000000000 | bytes 8388608 | tf_op jit(solution)/shard_map/attn_bwd/pallas_call | solution.py:383
  96.7 7.3 %mlp_bwd.1 = (f32[1024,256]{1,0:T(8,128)S(1)}, bf16[4,256,256]{2,1,0:T(8,128)(2,1)S(1)}, bf16[4,256,256]{2,1,0:T(8,128)(2,1)S(1)}, f32[8,256]{1,0:T(8,128)S(1)}) custom-call(s32[3]{0:T(128)S(1)} %pad_add_fusion.info, f32[1024,256]{1,0:T(8,128)S(1)} %get-tuple-element.53.grad_ref, f32[1024,256]{1,0:T(8,128)S(1)} %get-tuple-element.42.middle_ref, ...), custom_call_target="tpu_custom_call" | custom-call | flops 4000000000 | bytes 8388608 | tf_op jit(solution)/shard_map/mlp_bwd/pallas_call | solution.py:360
  104.0 14.7 %attn_bwd.3 = (f32[1024,256]{1,0:T(8,128)}, bf16[4,160,256]{2,1,0:T(8,128)(2,1)S(1)}, bf16[4,160,256]{2,1,0:T(8,128)(2,1)S(1)}, f32[8,256]{1,0:T(8,128)S(1)}) custom-call(s32[3]{0:T(128)S(1)} %pad_add_fusion.info, s32[16]{0:T(128)S(1)} %copy-done.14, f32[1024,256]{1,0:T(8,128)S(1)} %get-tuple-element.53.grad_ref, f32[1024,256]{1,0:T(8,128)S(1)} %get-tuple-element.56.gm_ref, ...), custom_call_target="tpu_custom_call" | custom-call | flops 4000000000 | bytes 8388608 | tf_op jit(solution)/shard_map/attn_bwd/pallas_call | solution.py:383
  120.0 0.8 collective-permute-done.24
  120.8 1.7 collective-permute-start.26
  122.5 1.0 collective-permute-start.27
  124.2 1.1 collective-permute-done.27
  125.3 1.2 collective-permute-start.28
  126.5 1.2 collective-permute-start.29
  127.9 2.6 %collective-permute-start.31 = (bf16[4,160,256]{2,1,0:T(8,128)(2,1)}, bf16[4,160,256]{2,1,0:T(8,128)(2,1)}, u32[]{:S(2)}, u32[]{:S(2)}) collective-permute-start(bf16[4,160,256]{2,1,0:T(8,128)(2,1)} %copy-done.3), channel_id=1, source_target_pairs={{0,4},{4,0},{8,12},{12,8},{16,20},{20,16},{24,28},{28,24},{1,5},{5... | collective-permute-start | bytes 983048 | tf_op jit(solution)/shard_map/ppermute | solution.py:391
  131.0 1.1 collective-permute-start.55
  134.0 1.0 fusion.19
  135.1 1.6 collective-permute-start.32
  136.6 0.8 collective-permute-start.33
  137.9 1.0 fusion.23
  138.9 2.4 %collective-permute-start.40 = (bf16[160,256]{1,0:T(8,128)(2,1)S(1)}, bf16[160,256]{1,0:T(8,128)(2,1)S(1)}, u32[]{:S(2)}, u32[]{:S(2)}) collective-permute-start(bf16[160,256]{1,0:T(8,128)(2,1)S(1)} %get-tuple-element.83), channel_id=1, source_target_pairs={{0,1},{1,0},{2,3},{3,2},{4,5},{5,4},{6,7},{7,6},{8,9},{9,8},{10,11... | collective-permute-start | bytes 245768 | tf_op jit(solution)/shard_map/ppermute | solution.py:391
  141.3 0.8 collective-permute-start.41
  142.7 0.9 fusion.7
  144.3 3.5 %collective-permute-done.41 = bf16[160,256]{1,0:T(8,128)(2,1)S(1)} collective-permute-done((bf16[160,256]{1,0:T(8,128)(2,1)S(1)}, bf16[160,256]{1,0:T(8,128)(2,1)S(1)}, u32[]{:S(2)}, u32[]{:S(2)}) %collective-permute-start.41) | collective-permute-done | bytes 81952 | tf_op jit(solution)/shard_map/ppermute | solution.py:391
  148.3 3.0 %collective-permute-done.42 = bf16[160,256]{1,0:T(8,128)(2,1)S(1)} collective-permute-done((bf16[160,256]{1,0:T(8,128)(2,1)S(1)}, bf16[160,256]{1,0:T(8,128)(2,1)S(1)}, u32[]{:S(2)}, u32[]{:S(2)}) %collective-permute-start.42) | collective-permute-done | bytes 81952 | tf_op jit(solution)/shard_map/ppermute | solution.py:391
  151.3 0.9 fusion.5
  153.0 2.0 collective-permute-start.44
  155.6 0.9 collective-permute-done.43
  156.4 5.5 %collective-permute-start.38 = (bf16[160,256]{1,0:T(8,128)(2,1)S(1)}, bf16[160,256]{1,0:T(8,128)(2,1)S(1)}, u32[]{:S(2)}, u32[]{:S(2)}) collective-permute-start(bf16[160,256]{1,0:T(8,128)(2,1)S(1)} %add_convert_fusion.15), channel_id=1, source_target_pairs={{0,4},{4,0},{8,12},{12,8},{16,20},{20,16},{24,28},{28,24},{1,5},{5... | collective-permute-start | bytes 245768 | tf_op jit(solution)/shard_map/ppermute | solution.py:391
  162.0 3.2 %collective-permute-start.46 = (bf16[160,256]{1,0:T(8,128)(2,1)S(1)}, bf16[160,256]{1,0:T(8,128)(2,1)S(1)}, u32[]{:S(2)}, u32[]{:S(2)}) collective-permute-start(bf16[160,256]{1,0:T(8,128)(2,1)S(1)} %add_convert_fusion.10), channel_id=1, source_target_pairs={{0,4},{4,0},{8,12},{12,8},{16,20},{20,16},{24,28},{28,24},{1,5},{5... | collective-permute-start | bytes 245768 | tf_op jit(solution)/shard_map/ppermute | solution.py:391
  165.2 1.1 fusion.9
  167.1 1.3 collective-permute-start.49
  169.2 1.6 collective-permute-start.56
  170.9 0.8 collective-permute-start.57
  174.9 6.3 %collective-permute-done.50 = bf16[256,256]{1,0:T(8,128)(2,1)S(1)} collective-permute-done((bf16[256,256]{1,0:T(8,128)(2,1)S(1)}, bf16[256,256]{1,0:T(8,128)(2,1)S(1)}, u32[]{:S(2)}, u32[]{:S(2)}) %collective-permute-start.50) | collective-permute-done | bytes 131104 | tf_op jit(solution)/shard_map/ppermute | solution.py:391
  181.2 1.0 fusion.3
  182.2 7.7 %collective-permute-start.51 = (bf16[256,256]{1,0:T(8,128)(2,1)S(1)}, bf16[256,256]{1,0:T(8,128)(2,1)S(1)}, u32[]{:S(2)}, u32[]{:S(2)}) collective-permute-start(bf16[256,256]{1,0:T(8,128)(2,1)S(1)} %fusion.3), channel_id=1, source_target_pairs={{0,8},{4,12},{8,0},{12,4},{16,24},{20,28},{24,16},{28,20},{1,9},{5... | collective-permute-start | bytes 393224 | tf_op jit(solution)/shard_map/ppermute | solution.py:391
  190.0 1.3 collective-permute-start.53
  191.2 0.9 collective-permute-done.58
  192.2 2.4 %collective-permute-start.59 = (bf16[256,256]{1,0:T(8,128)(2,1)S(1)}, bf16[256,256]{1,0:T(8,128)(2,1)S(1)}, u32[]{:S(2)}, u32[]{:S(2)}) collective-permute-start(bf16[256,256]{1,0:T(8,128)(2,1)S(1)} %fusion.1), channel_id=1, source_target_pairs={{0,8},{4,12},{8,0},{12,4},{16,24},{20,28},{24,16},{28,20},{1,9},{5... | collective-permute-start | bytes 393224 | tf_op jit(solution)/shard_map/ppermute | solution.py:391
  194.7 1.3 collective-permute-start.61
  196.3 3.2 %collective-permute-start.54 = (bf16[256,256]{1,0:T(8,128)(2,1)S(1)}, bf16[256,256]{1,0:T(8,128)(2,1)S(1)}, u32[]{:S(2)}, u32[]{:S(2)}) collective-permute-start(bf16[256,256]{1,0:T(8,128)(2,1)S(1)} %add_convert_fusion.5), channel_id=1, source_target_pairs={{0,4},{4,0},{8,12},{12,8},{16,20},{20,16},{24,28},{28,24},{1,5},{5... | collective-permute-start | bytes 393224 | tf_op jit(solution)/shard_map/ppermute | solution.py:391
  199.5 4.0 %collective-permute-done.60 = bf16[256,256]{1,0:T(8,128)(2,1)S(1)} collective-permute-done((bf16[256,256]{1,0:T(8,128)(2,1)S(1)}, bf16[256,256]{1,0:T(8,128)(2,1)S(1)}, u32[]{:S(2)}, u32[]{:S(2)}) %collective-permute-start.60) | collective-permute-done | bytes 131104 | tf_op jit(solution)/shard_map/ppermute | solution.py:391
  203.6 1.1 collective-permute-start.62
  204.7 1.0 collective-permute-done.62
  205.7 0.8 maximum_convert_fusion.1
  206.6 0.8 maximum_convert_fusion
  (163 shorter events, 19.4 us)
Async XLA Ops:
  3.2 33.4 %copy-start.14 = (s32[16]{0:T(128)S(1)}, s32[16]{0:T(128)}, u32[]{:S(2)}) copy-start(s32[16]{0:T(128)} %lens.7) | copy-start | bytes 196
  4.4 7.9 %collective-permute-start = (bf16[176,256]{1,0:T(8,128)(2,1)S(1)}, bf16[176,256]{1,0:T(8,128)(2,1)S(1)}, u32[]{:S(2)}, u32[]{:S(2)}) collective-permute-start(bf16[176,256]{1,0:T(8,128)(2,1)S(1)} %constant_dynamic-slice_fusion.2), channel_id=1, source_target_pairs={{0,1},{1,0},{2,3},{3,2},{4,5},{5,4},{6,7},{7,6},{8,9},{9,8},{10,11... | collective-permute-start | bytes 270344 | tf_op jit(solution)/shard_map/ppermute | solution.py:391
  4.4 9.0 %collective-permute-start.1 = (bf16[176,256]{1,0:T(8,128)(2,1)S(1)}, bf16[176,256]{1,0:T(8,128)(2,1)S(1)}, u32[]{:S(2)}, u32[]{:S(2)}) collective-permute-start(bf16[176,256]{1,0:T(8,128)(2,1)S(1)} %constant_dynamic-slice_fusion.2), channel_id=1, source_target_pairs={{0,2},{1,3},{2,0},{3,1},{4,6},{5,7},{6,4},{7,5},{8,10},{9,11},{10,... | collective-permute-start | bytes 270344 | tf_op jit(solution)/shard_map/ppermute | solution.py:391
  6.8 13.8 %collective-permute-start.2 = (bf16[176,256]{1,0:T(8,128)(2,1)S(1)}, bf16[176,256]{1,0:T(8,128)(2,1)S(1)}, u32[]{:S(2)}, u32[]{:S(2)}) collective-permute-start(bf16[176,256]{1,0:T(8,128)(2,1)S(1)} %constant_dynamic-slice_fusion.2), channel_id=1, source_target_pairs={{0,3},{1,2},{2,1},{3,0},{4,7},{5,6},{6,5},{7,4},{8,11},{9,10},{10,... | collective-permute-start | bytes 270344 | tf_op jit(solution)/shard_map/ppermute | solution.py:391
  8.5 22.0 %collective-permute-start.7 = (bf16[256,256]{1,0:T(8,128)(2,1)S(1)}, bf16[256,256]{1,0:T(8,128)(2,1)S(1)}, u32[]{:S(2)}, u32[]{:S(2)}) collective-permute-start(bf16[256,256]{1,0:T(8,128)(2,1)S(1)} %fusion.17), channel_id=1, source_target_pairs={{0,2},{1,3},{2,0},{3,1},{4,6},{5,7},{6,4},{7,5},{8,10},{9,11},{10,... | collective-permute-start | bytes 393224 | tf_op jit(solution)/shard_map/ppermute | solution.py:391
  11.8 18.9 %collective-permute-start.8 = (bf16[256,256]{1,0:T(8,128)(2,1)S(1)}, bf16[256,256]{1,0:T(8,128)(2,1)S(1)}, u32[]{:S(2)}, u32[]{:S(2)}) collective-permute-start(bf16[256,256]{1,0:T(8,128)(2,1)S(1)} %fusion.17), channel_id=1, source_target_pairs={{0,3},{1,2},{2,1},{3,0},{4,7},{5,6},{6,5},{7,4},{8,11},{9,10},{10,... | collective-permute-start | bytes 393224 | tf_op jit(solution)/shard_map/ppermute | solution.py:391
  12.2 18.7 %collective-permute-start.6 = (bf16[256,256]{1,0:T(8,128)(2,1)S(1)}, bf16[256,256]{1,0:T(8,128)(2,1)S(1)}, u32[]{:S(2)}, u32[]{:S(2)}) collective-permute-start(bf16[256,256]{1,0:T(8,128)(2,1)S(1)} %fusion.17), channel_id=1, source_target_pairs={{0,1},{1,0},{2,3},{3,2},{4,5},{5,4},{6,7},{7,6},{8,9},{9,8},{10,11... | collective-permute-start | bytes 393224 | tf_op jit(solution)/shard_map/ppermute | solution.py:391
  13.4 9.2 %collective-permute-start.12 = (bf16[176,256]{1,0:T(8,128)(2,1)S(1)}, bf16[176,256]{1,0:T(8,128)(2,1)S(1)}, u32[]{:S(2)}, u32[]{:S(2)}) collective-permute-start(bf16[176,256]{1,0:T(8,128)(2,1)S(1)} %constant_dynamic-slice_fusion.1), channel_id=1, source_target_pairs={{0,1},{1,0},{2,3},{3,2},{4,5},{5,4},{6,7},{7,6},{8,9},{9,8},{10,11... | collective-permute-start | bytes 270344 | tf_op jit(solution)/shard_map/ppermute | solution.py:391
  20.6 8.3 %collective-permute-start.13 = (bf16[176,256]{1,0:T(8,128)(2,1)S(1)}, bf16[176,256]{1,0:T(8,128)(2,1)S(1)}, u32[]{:S(2)}, u32[]{:S(2)}) collective-permute-start(bf16[176,256]{1,0:T(8,128)(2,1)S(1)} %constant_dynamic-slice_fusion.1), channel_id=1, source_target_pairs={{0,2},{1,3},{2,0},{3,1},{4,6},{5,7},{6,4},{7,5},{8,10},{9,11},{10,... | collective-permute-start | bytes 270344 | tf_op jit(solution)/shard_map/ppermute | solution.py:391
  22.6 12.4 %collective-permute-start.3 = (bf16[176,256]{1,0:T(8,128)(2,1)S(1)}, bf16[176,256]{1,0:T(8,128)(2,1)S(1)}, u32[]{:S(2)}, u32[]{:S(2)}) collective-permute-start(bf16[176,256]{1,0:T(8,128)(2,1)S(1)} %collective-permute-done.m1), channel_id=1, source_target_pairs={{0,4},{4,0},{8,12},{12,8},{16,20},{20,16},{24,28},{28,24},{1,5},{5... | collective-permute-start | bytes 270344 | tf_op jit(solution)/shard_map/ppermute | solution.py:391
  28.9 7.1 %collective-permute-start.4 = (bf16[176,256]{1,0:T(8,128)(2,1)S(1)}, bf16[176,256]{1,0:T(8,128)(2,1)S(1)}, u32[]{:S(2)}, u32[]{:S(2)}) collective-permute-start(bf16[176,256]{1,0:T(8,128)(2,1)S(1)} %collective-permute-done.1.m2), channel_id=1, source_target_pairs={{0,4},{4,0},{8,12},{12,8},{16,20},{20,16},{24,28},{28,24},{1,5},{5... | collective-permute-start | bytes 270344 | tf_op jit(solution)/shard_map/ppermute | solution.py:391
  30.5 5.6 %collective-permute-start.5 = (bf16[176,256]{1,0:T(8,128)(2,1)S(1)}, bf16[176,256]{1,0:T(8,128)(2,1)S(1)}, u32[]{:S(2)}, u32[]{:S(2)}) collective-permute-start(bf16[176,256]{1,0:T(8,128)(2,1)S(1)} %collective-permute-done.2.m3), channel_id=1, source_target_pairs={{0,4},{4,0},{8,12},{12,8},{16,20},{20,16},{24,28},{28,24},{1,5},{5... | collective-permute-start | bytes 270344 | tf_op jit(solution)/shard_map/ppermute | solution.py:391
  30.7 16.8 %collective-permute-start.14 = (bf16[176,256]{1,0:T(8,128)(2,1)S(1)}, bf16[176,256]{1,0:T(8,128)(2,1)S(1)}, u32[]{:S(2)}, u32[]{:S(2)}) collective-permute-start(bf16[176,256]{1,0:T(8,128)(2,1)S(1)} %constant_dynamic-slice_fusion.1), channel_id=1, source_target_pairs={{0,3},{1,2},{2,1},{3,0},{4,7},{5,6},{6,5},{7,4},{8,11},{9,10},{10,... | collective-permute-start | bytes 270344 | tf_op jit(solution)/shard_map/ppermute | solution.py:391
  31.0 16.5 %collective-permute-start.18 = (bf16[256,256]{1,0:T(8,128)(2,1)S(1)}, bf16[256,256]{1,0:T(8,128)(2,1)S(1)}, u32[]{:S(2)}, u32[]{:S(2)}) collective-permute-start(bf16[256,256]{1,0:T(8,128)(2,1)S(1)} %fusion.16), channel_id=1, source_target_pairs={{0,1},{1,0},{2,3},{3,2},{4,5},{5,4},{6,7},{7,6},{8,9},{9,8},{10,11... | collective-permute-start | bytes 393224 | tf_op jit(solution)/shard_map/ppermute | solution.py:391
  35.0 13.5 %collective-permute-start.10 = (bf16[256,256]{1,0:T(8,128)(2,1)S(1)}, bf16[256,256]{1,0:T(8,128)(2,1)S(1)}, u32[]{:S(2)}, u32[]{:S(2)}) collective-permute-start(bf16[256,256]{1,0:T(8,128)(2,1)S(1)} %collective-permute-done.7.m2), channel_id=1, source_target_pairs={{0,4},{4,0},{8,12},{12,8},{16,20},{20,16},{24,28},{28,24},{1,5},{5... | collective-permute-start | bytes 393224 | tf_op jit(solution)/shard_map/ppermute | solution.py:391
  36.0 13.1 %collective-permute-start.11 = (bf16[256,256]{1,0:T(8,128)(2,1)S(1)}, bf16[256,256]{1,0:T(8,128)(2,1)S(1)}, u32[]{:S(2)}, u32[]{:S(2)}) collective-permute-start(bf16[256,256]{1,0:T(8,128)(2,1)S(1)} %collective-permute-done.8.m3), channel_id=1, source_target_pairs={{0,4},{4,0},{8,12},{12,8},{16,20},{20,16},{24,28},{28,24},{1,5},{5... | collective-permute-start | bytes 393224 | tf_op jit(solution)/shard_map/ppermute | solution.py:391
  36.1 13.1 %collective-permute-start.9 = (bf16[256,256]{1,0:T(8,128)(2,1)S(1)}, bf16[256,256]{1,0:T(8,128)(2,1)S(1)}, u32[]{:S(2)}, u32[]{:S(2)}) collective-permute-start(bf16[256,256]{1,0:T(8,128)(2,1)S(1)} %collective-permute-done.6.m1), channel_id=1, source_target_pairs={{0,4},{4,0},{8,12},{12,8},{16,20},{20,16},{24,28},{28,24},{1,5},{5... | collective-permute-start | bytes 393224 | tf_op jit(solution)/shard_map/ppermute | solution.py:391
  47.5 9.9 %collective-permute-start.19 = (bf16[256,256]{1,0:T(8,128)(2,1)S(1)}, bf16[256,256]{1,0:T(8,128)(2,1)S(1)}, u32[]{:S(2)}, u32[]{:S(2)}) collective-permute-start(bf16[256,256]{1,0:T(8,128)(2,1)S(1)} %fusion.16), channel_id=1, source_target_pairs={{0,2},{1,3},{2,0},{3,1},{4,6},{5,7},{6,4},{7,5},{8,10},{9,11},{10,... | collective-permute-start | bytes 393224 | tf_op jit(solution)/shard_map/ppermute | solution.py:391
  47.5 13.0 %collective-permute-start.20 = (bf16[256,256]{1,0:T(8,128)(2,1)S(1)}, bf16[256,256]{1,0:T(8,128)(2,1)S(1)}, u32[]{:S(2)}, u32[]{:S(2)}) collective-permute-start(bf16[256,256]{1,0:T(8,128)(2,1)S(1)} %fusion.16), channel_id=1, source_target_pairs={{0,3},{1,2},{2,1},{3,0},{4,7},{5,6},{6,5},{7,4},{8,11},{9,10},{10,... | collective-permute-start | bytes 393224 | tf_op jit(solution)/shard_map/ppermute | solution.py:391
  48.5 12.9 %collective-permute-start.15 = (bf16[176,256]{1,0:T(8,128)(2,1)S(1)}, bf16[176,256]{1,0:T(8,128)(2,1)S(1)}, u32[]{:S(2)}, u32[]{:S(2)}) collective-permute-start(bf16[176,256]{1,0:T(8,128)(2,1)S(1)} %collective-permute-done.12.m1), channel_id=1, source_target_pairs={{0,4},{4,0},{8,12},{12,8},{16,20},{20,16},{24,28},{28,24},{1,5},{5... | collective-permute-start | bytes 270344 | tf_op jit(solution)/shard_map/ppermute | solution.py:391
  49.1 12.2 %collective-permute-start.16 = (bf16[176,256]{1,0:T(8,128)(2,1)S(1)}, bf16[176,256]{1,0:T(8,128)(2,1)S(1)}, u32[]{:S(2)}, u32[]{:S(2)}) collective-permute-start(bf16[176,256]{1,0:T(8,128)(2,1)S(1)} %collective-permute-done.13.m2), channel_id=1, source_target_pairs={{0,4},{4,0},{8,12},{12,8},{16,20},{20,16},{24,28},{28,24},{1,5},{5... | collective-permute-start | bytes 270344 | tf_op jit(solution)/shard_map/ppermute | solution.py:391
  49.2 12.2 %collective-permute-start.17 = (bf16[176,256]{1,0:T(8,128)(2,1)S(1)}, bf16[176,256]{1,0:T(8,128)(2,1)S(1)}, u32[]{:S(2)}, u32[]{:S(2)}) collective-permute-start(bf16[176,256]{1,0:T(8,128)(2,1)S(1)} %collective-permute-done.14.m3), channel_id=1, source_target_pairs={{0,4},{4,0},{8,12},{12,8},{16,20},{20,16},{24,28},{28,24},{1,5},{5... | collective-permute-start | bytes 270344 | tf_op jit(solution)/shard_map/ppermute | solution.py:391
  57.4 14.0 %collective-permute-start.21 = (bf16[256,256]{1,0:T(8,128)(2,1)S(1)}, bf16[256,256]{1,0:T(8,128)(2,1)S(1)}, u32[]{:S(2)}, u32[]{:S(2)}) collective-permute-start(bf16[256,256]{1,0:T(8,128)(2,1)S(1)} %collective-permute-done.18.m1), channel_id=1, source_target_pairs={{0,4},{4,0},{8,12},{12,8},{16,20},{20,16},{24,28},{28,24},{1,5},{5... | collective-permute-start | bytes 393224 | tf_op jit(solution)/shard_map/ppermute | solution.py:391
  60.5 10.9 %collective-permute-start.22 = (bf16[256,256]{1,0:T(8,128)(2,1)S(1)}, bf16[256,256]{1,0:T(8,128)(2,1)S(1)}, u32[]{:S(2)}, u32[]{:S(2)}) collective-permute-start(bf16[256,256]{1,0:T(8,128)(2,1)S(1)} %collective-permute-done.19.m2), channel_id=1, source_target_pairs={{0,4},{4,0},{8,12},{12,8},{16,20},{20,16},{24,28},{28,24},{1,5},{5... | collective-permute-start | bytes 393224 | tf_op jit(solution)/shard_map/ppermute | solution.py:391
  61.4 10.0 %collective-permute-start.23 = (bf16[256,256]{1,0:T(8,128)(2,1)S(1)}, bf16[256,256]{1,0:T(8,128)(2,1)S(1)}, u32[]{:S(2)}, u32[]{:S(2)}) collective-permute-start(bf16[256,256]{1,0:T(8,128)(2,1)S(1)} %collective-permute-done.20.m3), channel_id=1, source_target_pairs={{0,4},{4,0},{8,12},{12,8},{16,20},{20,16},{24,28},{28,24},{1,5},{5... | collective-permute-start | bytes 393224 | tf_op jit(solution)/shard_map/ppermute | solution.py:391
  119.4 1.4 collective-permute-start.24
  120.8 2.7 %collective-permute-start.25 = (f32[8,256]{1,0:T(8,128)S(1)}, f32[8,256]{1,0:T(8,128)S(1)}, u32[]{:S(2)}, u32[]{:S(2)}) collective-permute-start(f32[8,256]{1,0:T(8,128)S(1)} %add.178), channel_id=1, source_target_pairs={{0,1},{1,0},{2,3},{3,2},{4,5},{5,4},{6,7},{7,6},{8,9},{9,8},{10,11... | collective-permute-start | bytes 24584 | tf_op jit(solution)/shard_map/ppermute | solution.py:391
  120.8 3.4 %collective-permute-start.26 = (f32[8,256]{1,0:T(8,128)S(1)}, f32[8,256]{1,0:T(8,128)S(1)}, u32[]{:S(2)}, u32[]{:S(2)}) collective-permute-start(f32[8,256]{1,0:T(8,128)S(1)} %add.178), channel_id=1, source_target_pairs={{0,2},{1,3},{2,0},{3,1},{4,6},{5,7},{6,4},{7,5},{8,10},{9,11},{10,... | collective-permute-start | bytes 24584 | tf_op jit(solution)/shard_map/ppermute | solution.py:391
  122.5 2.8 %collective-permute-start.27 = (f32[8,256]{1,0:T(8,128)S(1)}, f32[8,256]{1,0:T(8,128)S(1)}, u32[]{:S(2)}, u32[]{:S(2)}) collective-permute-start(f32[8,256]{1,0:T(8,128)S(1)} %add.178), channel_id=1, source_target_pairs={{0,3},{1,2},{2,1},{3,0},{4,7},{5,6},{6,5},{7,4},{8,11},{9,10},{10,... | collective-permute-start | bytes 24584 | tf_op jit(solution)/shard_map/ppermute | solution.py:391
  125.3 5.2 %collective-permute-start.28 = (f32[8,256]{1,0:T(8,128)S(1)}, f32[8,256]{1,0:T(8,128)S(1)}, u32[]{:S(2)}, u32[]{:S(2)}) collective-permute-start(f32[8,256]{1,0:T(8,128)S(1)} %add_add_fusion.1), channel_id=1, source_target_pairs={{0,8},{4,12},{8,0},{12,4},{16,24},{20,28},{24,16},{28,20},{1,9},{5... | collective-permute-start | bytes 24584 | tf_op jit(solution)/shard_map/ppermute | solution.py:391
  126.5 4.5 %collective-permute-start.29 = (f32[8,256]{1,0:T(8,128)S(1)}, f32[8,256]{1,0:T(8,128)S(1)}, u32[]{:S(2)}, u32[]{:S(2)}) collective-permute-start(f32[8,256]{1,0:T(8,128)S(1)} %add_add_fusion.1), channel_id=1, source_target_pairs={{0,16},{4,20},{8,24},{12,28},{16,0},{20,4},{24,8},{28,12},{1,17},{... | collective-permute-start | bytes 24584 | tf_op jit(solution)/shard_map/ppermute | solution.py:391
  127.7 4.4 %collective-permute-start.30 = (f32[8,256]{1,0:T(8,128)S(1)}, f32[8,256]{1,0:T(8,128)S(1)}, u32[]{:S(2)}, u32[]{:S(2)}) collective-permute-start(f32[8,256]{1,0:T(8,128)S(1)} %add_add_fusion.1), channel_id=1, source_target_pairs={{0,24},{4,28},{8,16},{12,20},{16,8},{20,12},{24,0},{28,4},{1,25},{... | collective-permute-start | bytes 24584 | tf_op jit(solution)/shard_map/ppermute | solution.py:391
  127.9 6.1 %collective-permute-start.31 = (bf16[4,160,256]{2,1,0:T(8,128)(2,1)}, bf16[4,160,256]{2,1,0:T(8,128)(2,1)}, u32[]{:S(2)}, u32[]{:S(2)}) collective-permute-start(bf16[4,160,256]{2,1,0:T(8,128)(2,1)} %copy-done.3), channel_id=1, source_target_pairs={{0,4},{4,0},{8,12},{12,8},{16,20},{20,16},{24,28},{28,24},{1,5},{5... | collective-permute-start | bytes 983048 | tf_op jit(solution)/shard_map/ppermute | solution.py:391
  130.5 6.9 %collective-permute-start.39 = (bf16[4,160,256]{2,1,0:T(8,128)(2,1)}, bf16[4,160,256]{2,1,0:T(8,128)(2,1)}, u32[]{:S(2)}, u32[]{:S(2)}) collective-permute-start(bf16[4,160,256]{2,1,0:T(8,128)(2,1)} %copy-done.2), channel_id=1, source_target_pairs={{0,4},{4,0},{8,12},{12,8},{16,20},{20,16},{24,28},{28,24},{1,5},{5... | collective-permute-start | bytes 983048 | tf_op jit(solution)/shard_map/ppermute | solution.py:391
  130.5 34.7 %collective-permute-start.47 = (bf16[4,256,256]{2,1,0:T(8,128)(2,1)S(1)}, bf16[4,256,256]{2,1,0:T(8,128)(2,1)}, u32[]{:S(2)}, u32[]{:S(2)}) collective-permute-start(bf16[4,256,256]{2,1,0:T(8,128)(2,1)S(1)} %get-tuple-element.71), channel_id=1, source_target_pairs={{0,4},{4,0},{8,12},{12,8},{16,20},{20,16},{24,28},{28,24},{1,5},{5... | collective-permute-start | bytes 1572872 | tf_op jit(solution)/shard_map/ppermute | solution.py:391
  131.0 37.4 %collective-permute-start.55 = (bf16[4,256,256]{2,1,0:T(8,128)(2,1)S(1)}, bf16[4,256,256]{2,1,0:T(8,128)(2,1)S(1)}, u32[]{:S(2)}, u32[]{:S(2)}) collective-permute-start(bf16[4,256,256]{2,1,0:T(8,128)(2,1)S(1)} %get-tuple-element.73), channel_id=1, source_target_pairs={{0,4},{4,0},{8,12},{12,8},{16,20},{20,16},{24,28},{28,24},{1,5},{5... | collective-permute-start | bytes 1572872 | tf_op jit(solution)/shard_map/ppermute | solution.py:391
  135.1 3.9 %collective-permute-start.32 = (bf16[160,256]{1,0:T(8,128)(2,1)S(1)}, bf16[160,256]{1,0:T(8,128)(2,1)S(1)}, u32[]{:S(2)}, u32[]{:S(2)}) collective-permute-start(bf16[160,256]{1,0:T(8,128)(2,1)S(1)} %get-tuple-element.80), channel_id=1, source_target_pairs={{0,1},{1,0},{2,3},{3,2},{4,5},{5,4},{6,7},{7,6},{8,9},{9,8},{10,11... | collective-permute-start | bytes 245768 | tf_op jit(solution)/shard_map/ppermute | solution.py:391
  136.6 4.7 %collective-permute-start.33 = (bf16[160,256]{1,0:T(8,128)(2,1)S(1)}, bf16[160,256]{1,0:T(8,128)(2,1)S(1)}, u32[]{:S(2)}, u32[]{:S(2)}) collective-permute-start(bf16[160,256]{1,0:T(8,128)(2,1)S(1)} %get-tuple-element.82), channel_id=1, source_target_pairs={{0,2},{1,3},{2,0},{3,1},{4,6},{5,7},{6,4},{7,5},{8,10},{9,11},{10,... | collective-permute-start | bytes 245768 | tf_op jit(solution)/shard_map/ppermute | solution.py:391
  137.4 4.7 %collective-permute-start.34 = (bf16[160,256]{1,0:T(8,128)(2,1)S(1)}, bf16[160,256]{1,0:T(8,128)(2,1)S(1)}, u32[]{:S(2)}, u32[]{:S(2)}) collective-permute-start(bf16[160,256]{1,0:T(8,128)(2,1)S(1)} %get-tuple-element.81), channel_id=1, source_target_pairs={{0,3},{1,2},{2,1},{3,0},{4,7},{5,6},{6,5},{7,4},{8,11},{9,10},{10,... | collective-permute-start | bytes 245768 | tf_op jit(solution)/shard_map/ppermute | solution.py:391
  138.9 5.1 %collective-permute-start.40 = (bf16[160,256]{1,0:T(8,128)(2,1)S(1)}, bf16[160,256]{1,0:T(8,128)(2,1)S(1)}, u32[]{:S(2)}, u32[]{:S(2)}) collective-permute-start(bf16[160,256]{1,0:T(8,128)(2,1)S(1)} %get-tuple-element.83), channel_id=1, source_target_pairs={{0,1},{1,0},{2,3},{3,2},{4,5},{5,4},{6,7},{7,6},{8,9},{9,8},{10,11... | collective-permute-start | bytes 245768 | tf_op jit(solution)/shard_map/ppermute | solution.py:391
  141.3 6.4 %collective-permute-start.41 = (bf16[160,256]{1,0:T(8,128)(2,1)S(1)}, bf16[160,256]{1,0:T(8,128)(2,1)S(1)}, u32[]{:S(2)}, u32[]{:S(2)}) collective-permute-start(bf16[160,256]{1,0:T(8,128)(2,1)S(1)} %get-tuple-element.85), channel_id=1, source_target_pairs={{0,2},{1,3},{2,0},{3,1},{4,6},{5,7},{6,4},{7,5},{8,10},{9,11},{10,... | collective-permute-start | bytes 245768 | tf_op jit(solution)/shard_map/ppermute | solution.py:391
  142.1 9.2 %collective-permute-start.42 = (bf16[160,256]{1,0:T(8,128)(2,1)S(1)}, bf16[160,256]{1,0:T(8,128)(2,1)S(1)}, u32[]{:S(2)}, u32[]{:S(2)}) collective-permute-start(bf16[160,256]{1,0:T(8,128)(2,1)S(1)} %get-tuple-element.84), channel_id=1, source_target_pairs={{0,3},{1,2},{2,1},{3,0},{4,7},{5,6},{6,5},{7,4},{8,11},{9,10},{10,... | collective-permute-start | bytes 245768 | tf_op jit(solution)/shard_map/ppermute | solution.py:391
  144.0 8.2 %collective-permute-start.35 = (bf16[160,256]{1,0:T(8,128)(2,1)S(1)}, bf16[160,256]{1,0:T(8,128)(2,1)S(1)}, u32[]{:S(2)}, u32[]{:S(2)}) collective-permute-start(bf16[160,256]{1,0:T(8,128)(2,1)S(1)} %fusion.7), channel_id=1, source_target_pairs={{0,8},{4,12},{8,0},{12,4},{16,24},{20,28},{24,16},{28,20},{1,9},{5... | collective-permute-start | bytes 245768 | tf_op jit(solution)/shard_map/ppermute | solution.py:391
  147.7 5.3 %collective-permute-start.36 = (bf16[160,256]{1,0:T(8,128)(2,1)S(1)}, bf16[160,256]{1,0:T(8,128)(2,1)S(1)}, u32[]{:S(2)}, u32[]{:S(2)}) collective-permute-start(bf16[160,256]{1,0:T(8,128)(2,1)S(1)} %fusion.7), channel_id=1, source_target_pairs={{0,16},{4,20},{8,24},{12,28},{16,0},{20,4},{24,8},{28,12},{1,17},{... | collective-permute-start | bytes 245768 | tf_op jit(solution)/shard_map/ppermute | solution.py:391
  151.3 4.2 %collective-permute-start.37 = (bf16[160,256]{1,0:T(8,128)(2,1)S(1)}, bf16[160,256]{1,0:T(8,128)(2,1)S(1)}, u32[]{:S(2)}, u32[]{:S(2)}) collective-permute-start(bf16[160,256]{1,0:T(8,128)(2,1)S(1)} %fusion.7), channel_id=1, source_target_pairs={{0,24},{4,28},{8,16},{12,20},{16,8},{20,12},{24,0},{28,4},{1,25},{... | collective-permute-start | bytes 245768 | tf_op jit(solution)/shard_map/ppermute | solution.py:391
  152.2 4.2 %collective-permute-start.43 = (bf16[160,256]{1,0:T(8,128)(2,1)S(1)}, bf16[160,256]{1,0:T(8,128)(2,1)S(1)}, u32[]{:S(2)}, u32[]{:S(2)}) collective-permute-start(bf16[160,256]{1,0:T(8,128)(2,1)S(1)} %fusion.5), channel_id=1, source_target_pairs={{0,8},{4,12},{8,0},{12,4},{16,24},{20,28},{24,16},{28,20},{1,9},{5... | collective-permute-start | bytes 245768 | tf_op jit(solution)/shard_map/ppermute | solution.py:391
  153.0 9.0 %collective-permute-start.44 = (bf16[160,256]{1,0:T(8,128)(2,1)S(1)}, bf16[160,256]{1,0:T(8,128)(2,1)S(1)}, u32[]{:S(2)}, u32[]{:S(2)}) collective-permute-start(bf16[160,256]{1,0:T(8,128)(2,1)S(1)} %fusion.5), channel_id=1, source_target_pairs={{0,16},{4,20},{8,24},{12,28},{16,0},{20,4},{24,8},{28,12},{1,17},{... | collective-permute-start | bytes 245768 | tf_op jit(solution)/shard_map/ppermute | solution.py:391
  155.5 6.4 %collective-permute-start.45 = (bf16[160,256]{1,0:T(8,128)(2,1)S(1)}, bf16[160,256]{1,0:T(8,128)(2,1)S(1)}, u32[]{:S(2)}, u32[]{:S(2)}) collective-permute-start(bf16[160,256]{1,0:T(8,128)(2,1)S(1)} %fusion.5), channel_id=1, source_target_pairs={{0,24},{4,28},{8,16},{12,20},{16,8},{20,12},{24,0},{28,4},{1,25},{... | collective-permute-start | bytes 245768 | tf_op jit(solution)/shard_map/ppermute | solution.py:391
  156.4 12.7 %collective-permute-start.38 = (bf16[160,256]{1,0:T(8,128)(2,1)S(1)}, bf16[160,256]{1,0:T(8,128)(2,1)S(1)}, u32[]{:S(2)}, u32[]{:S(2)}) collective-permute-start(bf16[160,256]{1,0:T(8,128)(2,1)S(1)} %add_convert_fusion.15), channel_id=1, source_target_pairs={{0,4},{4,0},{8,12},{12,8},{16,20},{20,16},{24,28},{28,24},{1,5},{5... | collective-permute-start | bytes 245768 | tf_op jit(solution)/shard_map/ppermute | solution.py:391
  162.0 8.9 %collective-permute-start.46 = (bf16[160,256]{1,0:T(8,128)(2,1)S(1)}, bf16[160,256]{1,0:T(8,128)(2,1)S(1)}, u32[]{:S(2)}, u32[]{:S(2)}) collective-permute-start(bf16[160,256]{1,0:T(8,128)(2,1)S(1)} %add_convert_fusion.10), channel_id=1, source_target_pairs={{0,4},{4,0},{8,12},{12,8},{16,20},{20,16},{24,28},{28,24},{1,5},{5... | collective-permute-start | bytes 245768 | tf_op jit(solution)/shard_map/ppermute | solution.py:391
  166.4 7.5 %collective-permute-start.48 = (bf16[256,256]{1,0:T(8,128)(2,1)S(1)}, bf16[256,256]{1,0:T(8,128)(2,1)S(1)}, u32[]{:S(2)}, u32[]{:S(2)}) collective-permute-start(bf16[256,256]{1,0:T(8,128)(2,1)S(1)} %get-tuple-element.74), channel_id=1, source_target_pairs={{0,1},{1,0},{2,3},{3,2},{4,5},{5,4},{6,7},{7,6},{8,9},{9,8},{10,11... | collective-permute-start | bytes 393224 | tf_op jit(solution)/shard_map/ppermute | solution.py:391
  167.1 7.8 %collective-permute-start.49 = (bf16[256,256]{1,0:T(8,128)(2,1)S(1)}, bf16[256,256]{1,0:T(8,128)(2,1)S(1)}, u32[]{:S(2)}, u32[]{:S(2)}) collective-permute-start(bf16[256,256]{1,0:T(8,128)(2,1)S(1)} %get-tuple-element.76), channel_id=1, source_target_pairs={{0,2},{1,3},{2,0},{3,1},{4,6},{5,7},{6,4},{7,5},{8,10},{9,11},{10,... | collective-permute-start | bytes 393224 | tf_op jit(solution)/shard_map/ppermute | solution.py:391
  168.4 12.8 %collective-permute-start.50 = (bf16[256,256]{1,0:T(8,128)(2,1)S(1)}, bf16[256,256]{1,0:T(8,128)(2,1)S(1)}, u32[]{:S(2)}, u32[]{:S(2)}) collective-permute-start(bf16[256,256]{1,0:T(8,128)(2,1)S(1)} %get-tuple-element.75), channel_id=1, source_target_pairs={{0,3},{1,2},{2,1},{3,0},{4,7},{5,6},{6,5},{7,4},{8,11},{9,10},{10,... | collective-permute-start | bytes 393224 | tf_op jit(solution)/shard_map/ppermute | solution.py:391
  169.2 20.8 %collective-permute-start.56 = (bf16[256,256]{1,0:T(8,128)(2,1)S(1)}, bf16[256,256]{1,0:T(8,128)(2,1)S(1)}, u32[]{:S(2)}, u32[]{:S(2)}) collective-permute-start(bf16[256,256]{1,0:T(8,128)(2,1)S(1)} %get-tuple-element.77), channel_id=1, source_target_pairs={{0,1},{1,0},{2,3},{3,2},{4,5},{5,4},{6,7},{7,6},{8,9},{9,8},{10,11... | collective-permute-start | bytes 393224 | tf_op jit(solution)/shard_map/ppermute | solution.py:391
  170.9 20.3 %collective-permute-start.57 = (bf16[256,256]{1,0:T(8,128)(2,1)S(1)}, bf16[256,256]{1,0:T(8,128)(2,1)S(1)}, u32[]{:S(2)}, u32[]{:S(2)}) collective-permute-start(bf16[256,256]{1,0:T(8,128)(2,1)S(1)} %get-tuple-element.79), channel_id=1, source_target_pairs={{0,2},{1,3},{2,0},{3,1},{4,6},{5,7},{6,4},{7,5},{8,10},{9,11},{10,... | collective-permute-start | bytes 393224 | tf_op jit(solution)/shard_map/ppermute | solution.py:391
  173.9 18.2 %collective-permute-start.58 = (bf16[256,256]{1,0:T(8,128)(2,1)S(1)}, bf16[256,256]{1,0:T(8,128)(2,1)S(1)}, u32[]{:S(2)}, u32[]{:S(2)}) collective-permute-start(bf16[256,256]{1,0:T(8,128)(2,1)S(1)} %get-tuple-element.78), channel_id=1, source_target_pairs={{0,3},{1,2},{2,1},{3,0},{4,7},{5,6},{6,5},{7,4},{8,11},{9,10},{10,... | collective-permute-start | bytes 393224 | tf_op jit(solution)/shard_map/ppermute | solution.py:391
  182.2 12.5 %collective-permute-start.51 = (bf16[256,256]{1,0:T(8,128)(2,1)S(1)}, bf16[256,256]{1,0:T(8,128)(2,1)S(1)}, u32[]{:S(2)}, u32[]{:S(2)}) collective-permute-start(bf16[256,256]{1,0:T(8,128)(2,1)S(1)} %fusion.3), channel_id=1, source_target_pairs={{0,8},{4,12},{8,0},{12,4},{16,24},{20,28},{24,16},{28,20},{1,9},{5... | collective-permute-start | bytes 393224 | tf_op jit(solution)/shard_map/ppermute | solution.py:391
  190.0 6.0 %collective-permute-start.52 = (bf16[256,256]{1,0:T(8,128)(2,1)S(1)}, bf16[256,256]{1,0:T(8,128)(2,1)S(1)}, u32[]{:S(2)}, u32[]{:S(2)}) collective-permute-start(bf16[256,256]{1,0:T(8,128)(2,1)S(1)} %fusion.3), channel_id=1, source_target_pairs={{0,16},{4,20},{8,24},{12,28},{16,0},{20,4},{24,8},{28,12},{1,17},{... | collective-permute-start | bytes 393224 | tf_op jit(solution)/shard_map/ppermute | solution.py:391
  190.0 6.3 %collective-permute-start.53 = (bf16[256,256]{1,0:T(8,128)(2,1)S(1)}, bf16[256,256]{1,0:T(8,128)(2,1)S(1)}, u32[]{:S(2)}, u32[]{:S(2)}) collective-permute-start(bf16[256,256]{1,0:T(8,128)(2,1)S(1)} %fusion.3), channel_id=1, source_target_pairs={{0,24},{4,28},{8,16},{12,20},{16,8},{20,12},{24,0},{28,4},{1,25},{... | collective-permute-start | bytes 393224 | tf_op jit(solution)/shard_map/ppermute | solution.py:391
  192.2 7.3 %collective-permute-start.59 = (bf16[256,256]{1,0:T(8,128)(2,1)S(1)}, bf16[256,256]{1,0:T(8,128)(2,1)S(1)}, u32[]{:S(2)}, u32[]{:S(2)}) collective-permute-start(bf16[256,256]{1,0:T(8,128)(2,1)S(1)} %fusion.1), channel_id=1, source_target_pairs={{0,8},{4,12},{8,0},{12,4},{16,24},{20,28},{24,16},{28,20},{1,9},{5... | collective-permute-start | bytes 393224 | tf_op jit(solution)/shard_map/ppermute | solution.py:391
  194.7 8.9 %collective-permute-start.60 = (bf16[256,256]{1,0:T(8,128)(2,1)S(1)}, bf16[256,256]{1,0:T(8,128)(2,1)S(1)}, u32[]{:S(2)}, u32[]{:S(2)}) collective-permute-start(bf16[256,256]{1,0:T(8,128)(2,1)S(1)} %fusion.1), channel_id=1, source_target_pairs={{0,16},{4,20},{8,24},{12,28},{16,0},{20,4},{24,8},{28,12},{1,17},{... | collective-permute-start | bytes 393224 | tf_op jit(solution)/shard_map/ppermute | solution.py:391
  194.7 8.9 %collective-permute-start.61 = (bf16[256,256]{1,0:T(8,128)(2,1)S(1)}, bf16[256,256]{1,0:T(8,128)(2,1)S(1)}, u32[]{:S(2)}, u32[]{:S(2)}) collective-permute-start(bf16[256,256]{1,0:T(8,128)(2,1)S(1)} %fusion.1), channel_id=1, source_target_pairs={{0,24},{4,28},{8,16},{12,20},{16,8},{20,12},{24,0},{28,4},{1,25},{... | collective-permute-start | bytes 393224 | tf_op jit(solution)/shard_map/ppermute | solution.py:391
  196.3 8.4 %collective-permute-start.54 = (bf16[256,256]{1,0:T(8,128)(2,1)S(1)}, bf16[256,256]{1,0:T(8,128)(2,1)S(1)}, u32[]{:S(2)}, u32[]{:S(2)}) collective-permute-start(bf16[256,256]{1,0:T(8,128)(2,1)S(1)} %add_convert_fusion.5), channel_id=1, source_target_pairs={{0,4},{4,0},{8,12},{12,8},{16,20},{20,16},{24,28},{28,24},{1,5},{5... | collective-permute-start | bytes 393224 | tf_op jit(solution)/shard_map/ppermute | solution.py:391
  203.6 2.1 collective-permute-start.62
  (17 other events, 242.9 us)

commit v2 on v1

v2 whole, which is shorter than its diff:
```python
import functools

import jax
import jax.numpy as jnp
from jax import lax
from jax.experimental import pallas as pl
from jax.experimental.pallas import tpu as pltpu
from jax.sharding import PartitionSpec as P

HD = 64
LAYERS = 2
EPSILON = 1e-06
MASKED_SCORE = -1000000000.0
BF = jnp.bfloat16
F32 = jnp.float32

VMEM_LIMIT = 32 * 2**20
SMALL_LIMIT = 12 * 2**20
KERNEL_FLOPS = 1000


def nn(a, b):
    return lax.dot_general(a, b, (((1,), (0,)), ((), ())), preferred_element_type=F32)


def nt(a, b):
    return lax.dot_general(a, b, (((1,), (1,)), ((), ())), preferred_element_type=F32)


def tn(a, b):
    return lax.dot_general(a, b, (((0,), (0,)), ((), ())), preferred_element_type=F32)


def rescale_of(values):
    return lax.rsqrt(jnp.mean(values * values, axis=-1, keepdims=True) + EPSILON)


def norm_back(values, rescale, gain, gradient):
    scaled = gradient * gain
    product_mean = jnp.mean(values * scaled, axis=-1, keepdims=True)
    normal = values * rescale
    grad_values = rescale * (scaled - normal * (rescale * product_mean))
    return grad_values, jnp.sum(gradient * normal, axis=0, keepdims=True)


def gelu_and_slope(u):
    t = 1.0 / (1.0 + (0.3275911 * 0.7071067811865476) * jnp.abs(u))
    e = jnp.exp(-0.5 * (u * u))
    poly = ((((0.5 * 1.061405429) * t - 0.5 * 1.453152027) * t + 0.5 * 1.421413741) * t - 0.5 * 0.284496736) * t + 0.5 * 0.254829592
    tail = poly * t * e
    cdf = jnp.where(u >= 0.0, 1.0 - tail, tail)
    return u * cdf, cdf + u * (e * 0.3989422804014327)


def head_index():
    return lax.axis_index("head")


def half_index():
    return lax.axis_index("dp") & 1


def load_pieces(own, mine, theirs, dst, half_at, sem, first=0):
    half = dst.shape[1] // 2
    keep = pl.multiple_of(half_at * half, 16)
    other = pl.multiple_of((1 - half_at) * half, 16)
    copies = []
    at = 0
    for ref in own:
        copies.append(pltpu.make_async_copy(ref, dst.at[0, pl.ds(at, ref.shape[0])], sem))
        at += ref.shape[0]
    for m, ref in enumerate(mine):
        copies.append(pltpu.make_async_copy(ref.at[pl.ds(first, half)], dst.at[m + 1, pl.ds(keep, half)], sem))
    for m, ref in enumerate(theirs):
        copies.append(pltpu.make_async_copy(ref.at[pl.ds(first, half)], dst.at[m + 1, pl.ds(other, half)], sem))
    for copy in copies:
        copy.start()
    for copy in copies:
        copy.wait()


def spread_attn(wa, w_cross, w_out, bias, head_at, heads):
    total = jnp.zeros((1, 256), F32)
    for m in range(heads):
        place = pl.multiple_of((head_at ^ m) * HD, HD)
        w_cross[pl.ds(place, HD), :] = wa[m, 192:256, :]
        w_out[m * HD:(m + 1) * HD, :] = wa[m, 256:320, :]
        total = total + wa[m, 320:336, :].astype(F32)[0:1, :]
    bias[...] = jnp.broadcast_to(total, bias.shape)


def attn_fwd_kernel(layer, first, lens, cur_ref, gain_ref, own, m1, m2, m3, t1, t2, t3,
                    middle_ref, base_ref, nrm_ref, qkv_ref, mix_ref, lse_ref,
                    wa, w_cross, w_out, bias, sem):
    step = pl.program_id(0)

    @pl.when(step == 0)
    def _():
        load_pieces((own,), (m1, m2, m3), (t1, t2, t3), wa, half_index(), sem, first)
        spread_attn(wa, w_cross, w_out, bias, head_index(), 4)

    length = lens[head_index() * pl.num_programs(0) + step]
    cur = cur_ref[...].astype(F32)
    nrm = (cur * rescale_of(cur) * gain_ref[layer:layer + 1, :]).astype(BF)
    nrm_ref[...] = nrm
    slots = lax.broadcasted_iota(jnp.int32, (256, 256), 0)
    valid = slots < length
    for m in range(4):
        qkv = nt(wa[m, 0:192, :], nrm).astype(BF)
        qkv_ref[m * 192:(m + 1) * 192, :] = qkv
        scores = tn(qkv[64:128], qkv[0:64] * BF(0.125))
        scores = jnp.where(valid, scores, MASKED_SCORE)
        top = jnp.max(scores, axis=0, keepdims=True)
        e = jnp.exp(scores - top)
        total = jnp.sum(e, axis=0, keepdims=True)
        p = (e * (1.0 / total)).astype(BF)
        mix_ref[m * HD:(m + 1) * HD, :] = nn(qkv[128:192], p).astype(BF)
        lse_ref[m:m + 1, :] = top + jnp.log(total)
    middle = cur + tn(mix_ref[...], w_out[...])
    middle_ref[...] = middle
    cross = nt(nrm, w_cross[...]) + bias[0:1, :]
    base_ref[...] = middle + cur * cross


def mlp_fwd_block(middle, gain, wm):
    r = rescale_of(middle)
    n2 = (middle * r * gain).astype(BF)
    feed = None
    kept = []
    for m in range(4):
        u = nn(n2, wm[m, 0:256, :])
        hid, slope = gelu_and_slope(u)
        hid = hid.astype(BF)
        kept.append((hid, slope.astype(BF)))
        part = nn(hid, wm[m, 256:512, :])
        feed = part if feed is None else feed + part
    return r, n2, kept, feed


def mlp_fwd_kernel(layer, first, middle_ref, base_ref, gain_ref, up, down, m1, m2, m3, t1, t2, t3,
                   out_ref, hid_ref, slope_ref, wm, sem):
    @pl.when(pl.program_id(0) == 0)
    def _():
        load_pieces((up.at[layer], down.at[layer]), (m1, m2, m3), (t1, t2, t3), wm, half_index(), sem, first)

    _, _, kept, feed = mlp_fwd_block(middle_ref[...], gain_ref[layer:layer + 1, :], wm)
    for m, (hid, slope) in enumerate(kept):
        hid_ref[:, m * 256:(m + 1) * 256] = hid
        slope_ref[:, m * 256:(m + 1) * 256] = slope
    out_ref[...] = base_ref[...] + feed


def mlp_bwd_block(grad, middle, r, n2, kept, gain, wm, acc, small):
    gf = grad.astype(BF)
    gn = None
    for m in range(4):
        hid, slope = kept[m]
        gp = (nt(gf, wm[m, 256:512, :]) * slope.astype(F32)).astype(BF)
        acc[1, m] += tn(hid, gf)
        acc[0, m] += tn(n2, gp)
        part = nt(gp, wm[m, 0:256, :])
        gn = part if gn is None else gn + part
    back, gain_grad = norm_back(middle, r, gain, gn)
    small[0:1, :] += gain_grad
    return grad + back


def emit_mlp_grads(acc, keep_ref, send_ref):
    keep_ref[...] = acc[half_index()].astype(BF)
    send_ref[...] = acc[1 - half_index()].astype(BF)


def mlp_both_kernel(layer, first, middle_ref, base_ref, cot_ref, gain_ref, up, down, m1, m2, m3, t1, t2, t3,
                    out_ref, gm_ref, keep_ref, send_ref, small_ref, wm, acc, sem):
    step = pl.program_id(0)

    @pl.when(step == 0)
    def _():
        load_pieces((up.at[layer], down.at[layer]), (m1, m2, m3), (t1, t2, t3), wm, half_index(), sem, first)
        acc[...] = jnp.zeros_like(acc)
        small_ref[...] = jnp.zeros_like(small_ref)

    middle = middle_ref[...]
    gain = gain_ref[layer:layer + 1, :]
    r, n2, kept, feed = mlp_fwd_block(middle, gain, wm)
    out_ref[...] = base_ref[...] + feed
    grad = cot_ref[...].astype(F32)
    gm_ref[...] = mlp_bwd_block(grad, middle, r, n2, kept, gain, wm, acc, small_ref)

    @pl.when(step == pl.num_programs(0) - 1)
    def _():
        emit_mlp_grads(acc, keep_ref, send_ref)


def mlp_bwd_kernel(layer, first, grad_ref, middle_ref, hid_ref, slope_ref, gain_ref, up, down, m1, m2, m3, t1, t2, t3,
                   gm_ref, keep_ref, send_ref, small_ref, wm, acc, sem):
    step = pl.program_id(0)

    @pl.when(step == 0)
    def _():
        load_pieces((up.at[layer], down.at[layer]), (m1, m2, m3), (t1, t2, t3), wm, half_index(), sem, first)
        acc[...] = jnp.zeros_like(acc)
        small_ref[...] = jnp.zeros_like(small_ref)

    middle = middle_ref[...]
    gain = gain_ref[layer:layer + 1, :]
    r = rescale_of(middle)
    n2 = (middle * r * gain).astype(BF)
    kept = [(hid_ref[:, m * 256:(m + 1) * 256], slope_ref[:, m * 256:(m + 1) * 256]) for m in range(4)]
    gm_ref[...] = mlp_bwd_block(grad_ref[...], middle, r, n2, kept, gain, wm, acc, small_ref)

    @pl.when(step == pl.num_programs(0) - 1)
    def _():
        emit_mlp_grads(acc, keep_ref, send_ref)


def attn_bwd_kernel(layer, first, lens, grad_ref, gm_ref, cur_ref, nrm_ref, qkv_ref, mix_ref, lse_ref, gain_ref, mlp_small,
                    own, m1, m2, m3, t1, t2, t3,
                    out_ref, keep_ref, send_ref,
                    wa, w_cross, w_out, bias, d_qkv, d_cross, d_out, payload, small_ref, sem):
    step = pl.program_id(0)

    @pl.when(step == 0)
    def _():
        load_pieces((own,), (m1, m2, m3), (t1, t2, t3), wa, half_index(), sem, first)
        spread_attn(wa, w_cross, w_out, bias, head_index(), 4)
        d_qkv[...] = jnp.zeros_like(d_qkv)
        d_cross[...] = jnp.zeros_like(d_cross)
        d_out[...] = jnp.zeros_like(d_out)
        small_ref[...] = jnp.zeros_like(small_ref)
        small_ref[2:3, :] = mlp_small[0:1, :]

    length = lens[head_index() * pl.num_programs(0) + step]
    valid = lax.broadcasted_iota(jnp.int32, (256, 256), 0) < length
    grad = grad_ref[...].astype(F32)
    gm = gm_ref[...]
    cur = cur_ref[...].astype(F32)
    nrm = nrm_ref[...]
    ga = gm.astype(BF)
    d_out[...] += nn(mix_ref[...], ga)
    gmix = nt(w_out[...], ga).astype(BF)
    gc = (grad * cur).astype(BF)
    d_cross[...] += tn(gc, nrm)
    gn = nn(gc, w_cross[...])
    cross = nt(nrm, w_cross[...]) + bias[0:1, :]
    for m in range(4):
        q = qkv_ref[m * 192:m * 192 + 64, :]
        k = qkv_ref[m * 192 + 64:m * 192 + 128, :]
        v = qkv_ref[m * 192 + 128:m * 192 + 192, :]
        go = gmix[m * HD:(m + 1) * HD]
        scores = tn(k, q * BF(0.125))
        scores = jnp.where(valid, scores, MASKED_SCORE)
        p = jnp.exp(scores - lse_ref[m:m + 1, :])
        gv = nt(go, p.astype(BF))
        gp = tn(v, go)
        dot = jnp.sum(gp * p, axis=0, keepdims=True)
        gs = (p * (gp - dot)).astype(BF)
        gq = nn(k, gs) * 0.125
        gk = nt(q, gs) * 0.125
        gqkv = jnp.concatenate([gq, gk, gv], axis=0).astype(BF)
        d_qkv[m * 192:(m + 1) * 192, :] += nn(gqkv, nrm)
        gn = gn + tn(gqkv, wa[m, 0:192, :])
    r = rescale_of(cur)
    back, gain_grad = norm_back(cur, r, gain_ref[layer:layer + 1, :], gn)
    small_ref[0:1, :] += gain_grad
    small_ref[1:2, :] += jnp.sum(gc.astype(F32), axis=0, keepdims=True)
    out_ref[...] = gm + grad * cross + back

    @pl.when(step == pl.num_programs(0) - 1)
    def _():
        high, low = split_rows(small_ref[...])
        for m in range(4):
            place = pl.multiple_of((head_index() ^ m) * HD, HD)
            payload[m, 0:192, :] = d_qkv[m * 192:(m + 1) * 192, :].astype(BF)
            payload[m, 192:256, :] = d_cross[pl.ds(place, HD), :].astype(BF)
            payload[m, 256:320, :] = d_out[m * HD:(m + 1) * HD, :].astype(BF)
        keep = pl.multiple_of(half_index() * 160, 16)
        other = pl.multiple_of((1 - half_index()) * 160, 16)
        for m in range(4):
            for ref, at in ((keep_ref, keep), (send_ref, other)):
                ref[m, 0:160, :] = payload[m, pl.ds(at, 160), :]
                ref[m, 160:168, :] = high
                ref[m, 168:176, :] = low


def split_rows(x):
    high = x.astype(BF)
    return high, (x - high.astype(F32)).astype(BF)


def pack_kernel(qkv, cross, out, up, down, b, own0, own1, half_a0, half_r, half_m1, sems):
    copies = []
    for l, own in ((0, own0), (1, own1)):
        for t in range(3):
            copies.append(pltpu.make_async_copy(qkv.at[l, t], own.at[pl.ds(t * HD, HD)], sems.at[0]))
        copies.append(pltpu.make_async_copy(cross.at[l], own.at[pl.ds(192, HD)], sems.at[0]))
        copies.append(pltpu.make_async_copy(out.at[l], own.at[pl.ds(256, HD)], sems.at[0]))
    for copy in copies:
        copy.start()

    def mlp_half(weight):
        return (pltpu.make_async_copy(weight.at[0], half_r.at[pl.ds(0, 256)], sems.at[1]),
                pltpu.make_async_copy(weight.at[1], half_m1, sems.at[1]))

    @pl.when(half_index() == 0)
    def _():
        for copy in mlp_half(up):
            copy.start()

    @pl.when(half_index() != 0)
    def _():
        for copy in mlp_half(down):
            copy.start()

    lane = lax.broadcasted_iota(jnp.int32, (LAYERS, 256), 1) // HD
    wide = jnp.concatenate([b[...].astype(F32)] * 4, axis=1)
    wide = jnp.where(lane == head_index(), wide, 0.0)
    for l, own in ((0, own0), (1, own1)):
        own[320:352, :] = jnp.broadcast_to(wide[l:l + 1], (32, 256)).astype(BF)
    for copy in copies:
        copy.wait()
    at = pl.multiple_of(half_index() * 176, 16)
    half_a0[...] = own0[pl.ds(at, 176), :]
    half_r[256:432, :] = own1[pl.ds(at, 176), :]
    for copy in mlp_half(up):
        copy.wait()


def put_sum(out, at, small_at, rows, total):
    for low, high in ((0, small_at), (small_at + 16, rows)):
        if low < high:
            out[at + low:at + high, :] = total(low, high).astype(BF)
    if small_at < rows:
        both = total(small_at, small_at + 16)
        high, low = split_rows(both[0:8] + both[8:16])
        out[at + small_at:at + small_at + 8, :] = high
        out[at + small_at + 8:at + small_at + 16, :] = low


def core_sum_kernel(small_at, *refs):
    ins, outs = refs[:-4], refs[-4:]
    for m, out in enumerate(outs):
        at = 0
        for where, keep, got in zip(small_at, ins[0::2], ins[1::2]):
            rows = keep.shape[1]
            put_sum(out, at, where, rows, lambda i, j: keep[m, i:j].astype(F32) + got[m, i:j].astype(F32))
            at += rows


def four_sum_kernel(small_at, copied, *refs):
    done, refs, out = refs[:copied], refs[copied:-1], refs[-1]
    at = 0
    for ref in done:
        out[at:at + ref.shape[0], :] = ref[...]
        at += ref.shape[0]
    for i, where in enumerate(small_at):
        s, a, b, c = refs[4 * i:4 * i + 4]
        rows = s.shape[0]
        put_sum(out, at, where, rows, lambda i, j: (s[i:j].astype(F32) + a[i:j].astype(F32)) + (b[i:j].astype(F32) + c[i:j].astype(F32)))
        at += rows


def finish_kernel(early, early_other, late, late_other,
                  d_qkv, d_out, d_up, d_down, d_cross, gain_attn, gain_mlp, bias):
    def place(first, second, late_first, late_second):
        for l, a, b, at in ((1, first, second, 256), (0, late_first, late_second, 0)):
            d_qkv[l, 0] = a[at:at + 64].astype(F32)
            d_qkv[l, 1] = a[at + 64:at + 128].astype(F32)
            d_qkv[l, 2, 0:32] = a[at + 128:at + 160].astype(F32)
            d_qkv[l, 2, 32:64] = b[at:at + 32].astype(F32)
            d_cross[l] = b[at + 32:at + 96].astype(F32)
            d_out[l] = b[at + 96:at + 160].astype(F32)
        for l, at in ((1, 0), (0, 432)):
            d_up[l] = first[at:at + 256].astype(F32)
            d_down[l] = second[at:at + 256].astype(F32)

    @pl.when(half_index() == 0)
    def _():
        place(early, early_other, late, late_other)

    @pl.when(half_index() != 0)
    def _():
        place(early_other, early, late_other, late)

    for l, ref, at in ((0, late, 160), (1, early, 416)):
        rows = ref[at:at + 8].astype(F32) + ref[at + 8:at + 16].astype(F32)
        gain_attn[l:l + 1, :] = rows[0:1]
        gain_mlp[l:l + 1, :] = rows[2:3]
        total = jnp.zeros((1, HD), F32)
        for h in range(4):
            total = total + jnp.where(head_index() == h, rows[1:2, h * HD:(h + 1) * HD], 0.0)
        bias[l:l + 1, :] = total


SMEM = pl.BlockSpec(memory_space=pltpu.SMEM)
ANY = pl.BlockSpec(memory_space=pl.ANY)


def row_spec(width):
    return pl.BlockSpec((256, width), lambda s: (s, 0))


def col_spec(height):
    return pl.BlockSpec((height, 256), lambda s: (0, s))


def whole(shape):
    return pl.BlockSpec(shape, lambda s: (0,) * len(shape))


def call(kernel, rows, in_specs, outs, scratch, flops, name):
    shapes = [jax.ShapeDtypeStruct(shape, dtype) for shape, dtype, _ in outs]
    return pl.pallas_call(
        kernel,
        grid=(rows // 256,),
        in_specs=in_specs,
        out_specs=[spec for _, _, spec in outs],
        out_shape=shapes,
        scratch_shapes=scratch,
        compiler_params=pltpu.CompilerParams(vmem_limit_bytes=VMEM_LIMIT, dimension_semantics=("arbitrary",)),
        cost_estimate=pl.CostEstimate(flops=flops, bytes_accessed=1024, transcendentals=0),
        name=name,
    )


ATTN_SCRATCH = [
    pltpu.VMEM((4, 352, 256), BF),
    pltpu.VMEM((256, 256), BF),
    pltpu.VMEM((256, 256), BF),
    pltpu.VMEM((8, 256), F32),
]


def attn_fwd(layer, first, lens, cur, gain, pieces):
    rows = cur.shape[0]
    outs = [
        ((rows, 256), F32, row_spec(256)),
        ((rows, 256), F32, row_spec(256)),
        ((rows, 256), BF, row_spec(256)),
        ((768, rows), BF, col_spec(768)),
        ((256, rows), BF, col_spec(256)),
        ((8, rows), F32, col_spec(8)),
    ]
    return call(
        functools.partial(attn_fwd_kernel, layer, first), rows, [SMEM, row_spec(256), whole((LAYERS, 256))] + [ANY] * 7, outs,
        ATTN_SCRATCH + [pltpu.SemaphoreType.DMA], KERNEL_FLOPS, "attn_fwd",
    )(lens, cur, gain, *pieces)


def mlp_fwd(layer, first, middle, base, gain, pieces):
    rows = middle.shape[0]
    outs = [
        ((rows, 256), F32, row_spec(256)),
        ((rows, 1024), BF, row_spec(1024)),
        ((rows, 1024), BF, row_spec(1024)),
    ]
    return call(
        functools.partial(mlp_fwd_kernel, layer, first), rows, [row_spec(256), row_spec(256), whole((LAYERS, 256))] + [ANY] * 8, outs,
        [pltpu.VMEM((4, 512, 256), BF), pltpu.SemaphoreType.DMA], KERNEL_FLOPS, "mlp_fwd",
    )(middle, base, gain, *pieces)


MLP_GRADS = [
    ((4, 256, 256), BF, whole((4, 256, 256))),
    ((4, 256, 256), BF, whole((4, 256, 256))),
    ((8, 256), F32, whole((8, 256))),
]
MLP_SCRATCH = [
    pltpu.VMEM((4, 512, 256), BF),
    pltpu.VMEM((2, 4, 256, 256), F32),
    pltpu.SemaphoreType.DMA,
]


def mlp_both(layer, first, middle, base, cot, gain, pieces):
    rows = middle.shape[0]
    outs = [((rows, 256), F32, row_spec(256)), ((rows, 256), F32, row_spec(256))] + MLP_GRADS
    return call(
        functools.partial(mlp_both_kernel, layer, first), rows, [row_spec(256)] * 3 + [whole((LAYERS, 256))] + [ANY] * 8, outs,
        MLP_SCRATCH, KERNEL_FLOPS, "mlp_both",
    )(middle, base, cot, gain, *pieces)


def mlp_bwd(layer, first, grad, middle, hid, slope, gain, pieces):
    rows = middle.shape[0]
    outs = [((rows, 256), F32, row_spec(256))] + MLP_GRADS
    return call(
        functools.partial(mlp_bwd_kernel, layer, first), rows,
        [row_spec(256), row_spec(256), row_spec(1024), row_spec(1024), whole((LAYERS, 256))] + [ANY] * 8, outs,
        MLP_SCRATCH, KERNEL_FLOPS, "mlp_bwd",
    )(grad, middle, hid, slope, gain, *pieces)


def attn_bwd(layer, first, lens, grad, gm, cur, saved, gain, mlp_small, pieces):
    nrm, qkv, mix, lse = saved
    rows = cur.shape[0]
    outs = [
        ((rows, 256), F32, row_spec(256)),
        ((4, 176, 256), BF, whole((4, 176, 256))),
        ((4, 176, 256), BF, whole((4, 176, 256))),
    ]
    scratch = ATTN_SCRATCH + [
        pltpu.VMEM((768, 256), F32),
        pltpu.VMEM((256, 256), F32),
        pltpu.VMEM((256, 256), F32),
        pltpu.VMEM((4, 320, 256), BF),
        pltpu.VMEM((8, 256), F32),
        pltpu.SemaphoreType.DMA,
    ]
    return call(
        functools.partial(attn_bwd_kernel, layer, first), rows,
        [SMEM] + [row_spec(256)] * 4 + [col_spec(768), col_spec(256), col_spec(8), whole((LAYERS, 256)), whole((8, 256))] + [ANY] * 7, outs,
        scratch, KERNEL_FLOPS, "attn_bwd",
    )(lens, grad, gm, cur, nrm, qkv, mix, lse, gain, mlp_small, *pieces)


VMEM = pl.BlockSpec(memory_space=pltpu.VMEM)


def small_call(kernel, shapes, name):
    def run(*args):
        return pl.pallas_call(
            kernel,
            in_specs=[VMEM] * len(args),
            out_specs=[VMEM] * len(shapes),
            out_shape=[jax.ShapeDtypeStruct(shape, dtype) for shape, dtype in shapes],
            compiler_params=pltpu.CompilerParams(vmem_limit_bytes=SMALL_LIMIT),
            cost_estimate=pl.CostEstimate(flops=1000, bytes_accessed=1024, transcendentals=0),
            name=name,
        )(*args)
    return run


def core_sum(small_at, *groups):
    rows = sum(keep.shape[1] for keep, _ in groups)
    return small_call(functools.partial(core_sum_kernel, small_at), [((rows, 256), BF)] * 4, "core_sum")(
        *[x for group in groups for x in group])


def four_sum(small_at, *groups, done=()):
    rows = sum(x.shape[0] for x in done) + sum(group[0].shape[0] for group in groups)
    return small_call(functools.partial(four_sum_kernel, small_at, len(done)), [((rows, 256), BF)], "four_sum")(
        *done, *[x for group in groups for x in group])[0]


def swap(x, axis, size, mask):
    return lax.ppermute(x, axis, [(i, i ^ mask) for i in range(size)])


def tie(x, *before):
    return lax.optimization_barrier((x,) + before)[0]


def solution(mesh):
    dp_size, head_size = mesh.shape["dp"], mesh.shape["head"]

    def core_swap(x):
        return swap(x, "dp", dp_size, 1)

    def fetch(x):
        return [swap(x, "head", head_size, m) for m in range(1, head_size)]

    def scatter(sums):
        return [sums[0]] + [swap(sums[m], "head", head_size, m) for m in range(1, head_size)]

    def spread(x, bit):
        return [x] + [swap(x, "dp", dp_size, m * bit) for m in (1, 2, 3)]

    def sum_rest(x, small_at, before=()):
        bit = 2
        while bit < dp_size:
            if bit * 2 < dp_size:
                x = four_sum((small_at,), [tie(term, *before) for term in spread(x, bit)])
            else:
                x = four_sum((small_at,), [x, swap(x, "dp", dp_size, bit), jnp.zeros_like(x), jnp.zeros_like(x)])
            bit *= 4
        return x

    def body(tokens, lengths, cotangent, gain_attn, gain_mlp, w_qkv, w_out, w_up, w_down, w_cross, b_cross):
        own0, own1, half_a0, half_r, half_m1 = pl.pallas_call(
            pack_kernel,
            in_specs=[ANY] * 5 + [VMEM],
            out_specs=[VMEM] * 5,
            out_shape=[jax.ShapeDtypeStruct((n, 256), BF) for n in (352, 352, 176, 432, 256)],
            scratch_shapes=[pltpu.SemaphoreType.DMA((2,))],
            name="pack",
        )(w_qkv.transpose(0, 2, 3, 1), w_cross.transpose(0, 2, 1), w_out, w_up, w_down, b_cross)

        a0 = fetch(half_a0)
        r = fetch(half_r)
        m1 = fetch(half_m1)
        pieces_a0 = [own0] + a0 + [core_swap(x) for x in a0]
        mid0, base0, *saved0 = attn_fwd(0, 0, lengths, tokens, gain_attn, pieces_a0)
        r = [tie(x, mid0) for x in r]
        r = r + [core_swap(x) for x in r]
        cur1, hid0, slope0 = mlp_fwd(0, 0, mid0, base0, gain_mlp, [w_up, w_down] + r)
        mid1, base1, *saved1 = attn_fwd(1, 256, lengths, cur1, gain_attn, [own1] + r)
        m1 = [tie(x, mid1) for x in m1]
        m1 = m1 + [core_swap(x) for x in m1]
        output, gm1, keep_m1, send_m1, small_m1 = mlp_both(1, 0, mid1, base1, cotangent, gain_mlp, [w_up, w_down] + m1)
        sums_m1 = core_sum((256,), (keep_m1, core_swap(send_m1)))
        got_m1 = scatter(sums_m1)
        grad1, keep_a1, send_a1 = attn_bwd(
            1, 256, lengths, cotangent, tie(gm1, *sums_m1), cur1, saved1, gain_attn, small_m1, [own1] + r)
        early = four_sum((256,), [tie(x, grad1) for x in got_m1])
        got_a1 = core_swap(send_a1)
        gm0, keep_m0, send_m0, small_m0 = mlp_bwd(0, 0, tie(grad1, early), mid0, hid0, slope0, gain_mlp, [w_up, w_down] + r)
        sums = core_sum((160, 256), (keep_a1, tie(got_a1, gm0)), (keep_m0, core_swap(send_m0)))
        got = scatter(sums)
        grad0, keep_a0, send_a0 = attn_bwd(
            0, 0, lengths, grad1, tie(gm0, *sums), tokens, saved0, gain_attn, small_m0, pieces_a0)
        early = four_sum((160,), [tie(x, grad0) for x in got], done=(early,))
        sums_a0 = core_sum((160,), (keep_a0, core_swap(tie(send_a0, early))))
        late = scatter(sums_a0)
        early = sum_rest(early, 416, late[1:])
        late = four_sum((160,), late)
        late = sum_rest(late, 160)
        d_qkv, d_out, d_up, d_down, d_cross, d_ga, d_gm, d_bias = small_call(
            finish_kernel,
            [((LAYERS, 3, HD, 256), F32), ((LAYERS, HD, 256), F32), ((LAYERS, 256, 256), F32), ((LAYERS, 256, 256), F32),
             ((LAYERS, HD, 256), F32), ((LAYERS, 256), F32), ((LAYERS, 256), F32), ((LAYERS, HD), F32)],
            "finish",
        )(early, core_swap(early), late, core_swap(late))
        return (output, grad0, d_ga, d_gm, d_qkv.transpose(0, 3, 1, 2), d_out, d_up, d_down,
                d_cross.transpose(0, 2, 1), d_bias)

    rows, weights = P(("dp", "head"), None), P(None, "head", None)
    return jax.shard_map(
        body,
        mesh=mesh,
        in_specs=(rows, P("dp"), rows, P(), P(), P(None, None, None, "head"), weights, P(None, None, "head"),
                  weights, P(None, None, "head"), P(None, "head")),
        out_specs=(rows, rows, P(), P(), P(None, None, None, "head"), weights, P(None, None, "head"),
                   weights, P(None, None, "head"), P(None, "head")),
        check_vma=False,
    )
```

time: 208 us -> 153 us (0.74)
  starting transfers between devices: 72.9 us -> 35 us
  other arithmetic: 11.1 us -> 0 us
  local copies, waits for them, and re-layouts: 9.65 us -> 3.34 us
    ppermute x63 -> x39, starting transfers between devices: 72.9 us -> 35 us  [swap(): return lax.ppermute(x, axis, [(i, i ^ mask) for i in range(size)])]
    convert_element_type x14 -> x0, other arithmetic: 6.53 us -> none  [the longest x4 3.26 us: reduce_pieces(): sums = [add(keep[m], got[m]).astype(BF) for m in range(head_size)]]
    another operation x8 -> x0, other arithmetic: 3.88 us -> none  [the longest x3 0.87 us: body(): d_down = jnp.stack([m0[1], m1[1]])]
    slice x11 -> x0, local copies, waits for them, and re-layouts: 2.91 us -> none  [the longest x1 0.95 us: body(): w_qkv[l].transpose(1, 2, 0).reshape(3 * HD, 256)]
    pallas_call x7 -> x17, Pallas kernels: 73.8 us -> 75.1 us  [the longest x2 28 us: attn_bwd(): call(functools.partial(attn_bwd_kernel, layer, first), rows, [SMEM] + [ro...]
    ppermute x63 -> x39, waiting for transfers between devices: 38.6 us -> 38.2 us  [swap(): return lax.ppermute(x, axis, [(i, i ^ mask) for i in range(size)])]
  transfers between devices with their start and end apart: 63 -> 39, of which waited for: 18 -> 17; matrix products, arithmetic and copies ran while one was open for 6% -> 0% of each run, Pallas kernels for 13% -> 36%
where the time goes in v2:
time: 153 us
  Pallas kernels  75.1 us (49%)
  waiting for transfers between devices  38.2 us (25%)
  starting transfers between devices  35 us (23%)
  local copies, waits for them, and re-layouts  3.34 us (2%)
    ppermute x39, waiting for transfers between devices, swap(): return lax.ppermute(x, axis, [(i, i ^ mask) for i in range(size)])  38.2 us
    ppermute x39, starting transfers between devices, swap(): return lax.ppermute(x, axis, [(i, i ^ mask) for i in range(size)])  35 us
    pallas_call x2, Pallas kernels, attn_bwd(): call(functools.partial(attn_bwd_kernel, layer, first), rows, [SMEM] + [ro...  28 us
    pallas_call x2, Pallas kernels, attn_fwd(): call(functools.partial(attn_fwd_kernel, layer, first), rows, [SMEM, row_s...  19.6 us
    pallas_call x1, Pallas kernels, mlp_both(): call(functools.partial(mlp_both_kernel, layer, first), rows, [row_spec(25...  10.2 us
    pallas_call x1, Pallas kernels, mlp_fwd(): call(functools.partial(mlp_fwd_kernel, layer, first), rows, [row_spec(256...  6.52 us
    pallas_call x1, Pallas kernels, mlp_bwd(): call(functools.partial(mlp_bwd_kernel, layer, first), rows, [row_spec(256...  5.94 us
    unnamed x24, local copies, waits for them, and re-layouts  3.34 us
  transfers between devices with their start and end apart: 39, of which 17 were waited for; matrix products, arithmetic and copies ran while one was open for 0% of the time, Pallas kernels for 36%

profile of v2, /device:TPU:9, one launch (start us, length us, event | category | flops | bytes accessed | tf_op | source)
XLA Modules:
  0.0 152.5 jit_solution(6435049480935816964)
XLA Ops:
  0.7 2.8 %pack.1 = (bf16[352,256]{1,0:T(8,128)(2,1)}, bf16[352,256]{1,0:T(8,128)(2,1)}, bf16[176,256]{1,0:T(8,128)(2,1)}, bf16[432,256]{1,0:T(8,128)(2,1)}, bf16[256,256]{1,0:T(8,128)(2,1)}) custom-call(bf16[2,3,64,256]{3,2,1,0:T(8,128)(2,1)} %bitcast.4, bf16[2,64,256]{2,1,0:T(8,128)(2,1)} %bitcast.5, bf16[2,64,256]{2,1,0:T(8,128)(2,1)} %out.1, ...), custom_call_target="tpu_custom_call" | custom-call | tf_op jit(solution)/shard_map/pack/pallas_call | solution.py:580
  3.4 1.4 collective-permute-start.2
  4.8 2.2 %collective-permute-start.6 = (bf16[432,256]{1,0:T(8,128)(2,1)}, bf16[432,256]{1,0:T(8,128)(2,1)S(1)}, u32[]{:S(2)}, u32[]{:S(2)}) collective-permute-start(bf16[432,256]{1,0:T(8,128)(2,1)} %get-tuple-element.92), channel_id=1, source_target_pairs={{0,1},{1,0},{2,3},{3,2},{4,5},{5,4},{6,7},{7,6},{8,9},{9,8},{10,11... | collective-permute-start | bytes 663560 | tf_op jit(solution)/shard_map/ppermute | solution.py:547
  7.0 0.4 collective-permute-start
  7.4 0.9 collective-permute-done.2.m3
  8.3 2.8 %collective-permute-start.5 = (bf16[176,256]{1,0:T(8,128)(2,1)S(1)}, bf16[176,256]{1,0:T(8,128)(2,1)S(1)}, u32[]{:S(2)}, u32[]{:S(2)}) collective-permute-start(bf16[176,256]{1,0:T(8,128)(2,1)S(1)} %collective-permute-done.2.m3), channel_id=1, source_target_pairs={{0,4},{4,0},{8,12},{12,8},{16,20},{20,16},{24,28},{28,24},{1,5},{5... | collective-permute-start | bytes 270344 | tf_op jit(solution)/shard_map/ppermute | solution.py:547
  11.0 0.4 collective-permute-start.8
  11.4 3.6 %collective-permute-done.1.m2 = bf16[176,256]{1,0:T(8,128)(2,1)S(1)} collective-permute-done((bf16[176,256]{1,0:T(8,128)(2,1)}, bf16[176,256]{1,0:T(8,128)(2,1)S(1)}, u32[]{:S(2)}, u32[]{:S(2)}) %collective-permute-start.1) | collective-permute-done | bytes 90144 | tf_op jit(solution)/shard_map/ppermute | solution.py:547
  15.1 2.7 %collective-permute-done.m1 = bf16[176,256]{1,0:T(8,128)(2,1)S(1)} collective-permute-done((bf16[176,256]{1,0:T(8,128)(2,1)}, bf16[176,256]{1,0:T(8,128)(2,1)S(1)}, u32[]{:S(2)}, u32[]{:S(2)}) %collective-permute-start) | collective-permute-done | bytes 90144 | tf_op jit(solution)/shard_map/ppermute | solution.py:547
  17.8 2.7 %collective-permute-start.4 = (bf16[176,256]{1,0:T(8,128)(2,1)S(1)}, bf16[176,256]{1,0:T(8,128)(2,1)S(1)}, u32[]{:S(2)}, u32[]{:S(2)}) collective-permute-start(bf16[176,256]{1,0:T(8,128)(2,1)S(1)} %collective-permute-done.1.m2), channel_id=1, source_target_pairs={{0,4},{4,0},{8,12},{12,8},{16,20},{20,16},{24,28},{28,24},{1,5},{5... | collective-permute-start | bytes 270344 | tf_op jit(solution)/shard_map/ppermute | solution.py:547
  20.5 0.9 collective-permute-done.4.t2
  21.5 0.4 collective-permute-done.3.t1
  21.8 1.0 copy-done.3
  22.9 0.9 copy-done.5
  23.8 0.7 copy-done.8
  24.5 0.7 copy-done.11
  25.1 9.8 %attn_fwd.2 = (f32[1024,256]{1,0:T(8,128)S(1)}, f32[1024,256]{1,0:T(8,128)S(1)}, bf16[1024,256]{1,0:T(8,128)(2,1)S(1)}, bf16[768,1024]{1,0:T(8,128)(2,1)S(1)}, b...) custom-call(s32[16]{0:T(128)S(1)} %copy-done.11, bf16[1024,256]{1,0:T(8,128)(2,1)S(1)} %copy-done.3, ...), custom_call_target="tpu_custom_call" | custom-call | flops 1000 | bytes 1024 | tf_op jit(solution)/shard_map/attn_fwd/pallas_call | solution.py:444
  34.9 0.2 collective-permute-start.9
  35.1 0.4 collective-permute-start.10
  35.5 0.2 collective-permute-start.11
  35.7 5.2 %collective-permute-start.13 = (bf16[256,256]{1,0:T(8,128)(2,1)}, bf16[256,256]{1,0:T(8,128)(2,1)S(1)}, u32[]{:S(2)}, u32[]{:S(2)}) collective-permute-start(bf16[256,256]{1,0:T(8,128)(2,1)} %get-tuple-element.100), channel_id=1, source_target_pairs={{0,2},{1,3},{2,0},{3,1},{4,6},{5,7},{6,4},{7,5},{8,10},{9,11},{10,... | collective-permute-start | bytes 393224 | tf_op jit(solution)/shard_map/ppermute | solution.py:547
  40.9 6.5 %mlp_fwd.1 = (f32[1024,256]{1,0:T(8,128)S(1)}, bf16[1024,1024]{1,0:T(8,128)(2,1)S(1)}, bf16[1024,1024]{1,0:T(8,128)(2,1)S(1)}) custom-call(f32[1024,256]{1,0:T(8,128)S(1)} %get-tuple-element.90.middle_ref, f32[1024,256]{1,0:T(8,128)S(1)} %get-tuple-element.91.base_ref, f32[2,256]{1,0:T(2,128)S(1)} %copy-done.10, bf16[2,256,256]{2,1,0:T(8,128)(2,1)S(1)} %copy-done, ...), custom_call_target="tpu_custom_call" | custom-call | flops 1000 | bytes 1024 | tf_op jit(solution)/shard_map/mlp_fwd/pallas_call | solution.py:457
  47.4 9.8 %attn_fwd.3 = (f32[1024,256]{1,0:T(8,128)S(1)}, f32[1024,256]{1,0:T(8,128)S(1)}, bf16[1024,256]{1,0:T(8,128)(2,1)S(1)}, bf16[768,1024]{1,0:T(8,128)(2,1)S(1)}, b...) custom-call(s32[16]{0:T(128)S(1)} %copy-done.11, f32[1024,256]{1,0:T(8,128)S(1)} %get-tuple-element.96.cur_ref, ...), custom_call_target="tpu_custom_call" | custom-call | flops 1000 | bytes 1024 | tf_op jit(solution)/shard_map/attn_fwd/pallas_call | solution.py:444
  57.3 1.0 collective-permute-start.15
  58.3 0.4 collective-permute-start.17
  58.8 0.5 collective-permute-done.15.t1
  59.2 0.4 collective-permute-done.16.t2
  59.6 0.2 collective-permute-done.17.t3
  59.8 10.2 %mlp_both.1 = (f32[1024,256]{1,0:T(8,128)}, f32[1024,256]{1,0:T(8,128)S(1)}, bf16[4,256,256]{2,1,0:T(8,128)(2,1)S(1)}, bf16[4,256,256]{2,1,0:T(8,128)(2,1)S(1)}, f32[8,256]{1,0:T(8,128)S(1)}) custom-call(f32[1024,256]{1,0:T(8,128)S(1)} %get-tuple-element.98.middle_ref, f32[1024,256]{1,0:T(8,128)S(1)} %get-tuple-element.99.base_ref, ...), custom_call_target="tpu_custom_call" | custom-call | flops 1000 | bytes 1024 | tf_op jit(solution)/shard_map/mlp_both/pallas_call | solution.py:478
  69.9 0.4 collective-permute-start.18
  70.3 1.6 %collective-permute-done.18.refs_1_ = bf16[4,256,256]{2,1,0:T(8,128)(2,1)S(1)} collective-permute-done((bf16[4,256,256]{2,1,0:T(8,128)(2,1)S(1)}, bf16[4,256,256]{2,1,0:T(8,128)(2,1)S(1)}, u32[]{:S(2)}, u32[]{:S(2)}) %collective-permute-start.18) | collective-permute-done | bytes 524320 | tf_op jit(solution)/shard_map/ppermute | solution.py:547
  71.9 0.1 core_sum.3
  72.0 1.8 %collective-permute-start.19 = (bf16[256,256]{1,0:T(8,128)(2,1)S(1)}, bf16[256,256]{1,0:T(8,128)(2,1)S(1)}, u32[]{:S(2)}, u32[]{:S(2)}) collective-permute-start(bf16[256,256]{1,0:T(8,128)(2,1)S(1)} %get-tuple-element.109), channel_id=1, source_target_pairs={{0,1},{1,0},{2,3},{3,2},{4,5},{5,4},{6,7},{7,6},{8,9},{9,8},{10,11... | collective-permute-start | bytes 393224 | tf_op jit(solution)/shard_map/ppermute | solution.py:547
  73.8 1.3 collective-permute-start.21
  75.1 13.6 %attn_bwd.2 = (f32[1024,256]{1,0:T(8,128)S(1)}, bf16[4,176,256]{2,1,0:T(8,128)(2,1)S(1)}, bf16[4,176,256]{2,1,0:T(8,128)(2,1)S(1)}) custom-call(s32[16]{0:T(128)S(1)} %copy-done.11, bf16[1024,256]{1,0:T(8,128)(2,1)S(1)} %copy-done.2, f32[1024,256]{1,0:T(8,128)S(1)} %get-tuple-element.112.gm_ref, f32[1024,256]{1,0:T(8,128)S(1)} %get-tuple-element.96.cur_ref, ...), custom_call_target="tpu_custom_call" | custom-call | flops 1000 | bytes 1024 | tf_op jit(solution)/shard_map/attn_bwd/pallas_call | solution.py:510
  88.8 5.9 %mlp_bwd.1 = (f32[1024,256]{1,0:T(8,128)S(1)}, bf16[4,256,256]{2,1,0:T(8,128)(2,1)S(1)}, bf16[4,256,256]{2,1,0:T(8,128)(2,1)S(1)}, f32[8,256]{1,0:T(8,128)S(1)}) custom-call(f32[1024,256]{1,0:T(8,128)S(1)} %get-tuple-element.123.grad_ref, f32[1024,256]{1,0:T(8,128)S(1)} %get-tuple-element.90.middle_ref, bf16[1024,1024]{1,0:T(8,128)(2,1)S(1)} %get-tuple-element.124.hid_ref, ...), custom_call_target="tpu_custom_call" | custom-call | flops 1000 | bytes 1024 | tf_op jit(solution)/shard_map/mlp_bwd/pallas_call | solution.py:487
  94.8 0.9 collective-permute-start.23
  95.8 2.0 %collective-permute-done.22.refs_1_ = bf16[4,176,256]{2,1,0:T(8,128)(2,1)S(1)} collective-permute-done((bf16[4,176,256]{2,1,0:T(8,128)(2,1)S(1)}, bf16[4,176,256]{2,1,0:T(8,128)(2,1)S(1)}, u32[]{:S(2)}, u32[]{:S(2)}) %collective-permute-start.22) | collective-permute-done | bytes 360480 | tf_op jit(solution)/shard_map/ppermute | solution.py:547
  97.8 0.2 core_sum.4
  98.0 2.6 %collective-permute-start.24 = (bf16[432,256]{1,0:T(8,128)(2,1)S(1)}, bf16[432,256]{1,0:T(8,128)(2,1)S(1)}, u32[]{:S(2)}, u32[]{:S(2)}) collective-permute-start(bf16[432,256]{1,0:T(8,128)(2,1)S(1)} %get-tuple-element.133), channel_id=1, source_target_pairs={{0,1},{1,0},{2,3},{3,2},{4,5},{5,4},{6,7},{7,6},{8,9},{9,8},{10,11... | collective-permute-start | bytes 663560 | tf_op jit(solution)/shard_map/ppermute | solution.py:547
  100.7 1.3 collective-permute-start.26
  101.9 14.3 %attn_bwd.3 = (f32[1024,256]{1,0:T(8,128)}, bf16[4,176,256]{2,1,0:T(8,128)(2,1)S(1)}, bf16[4,176,256]{2,1,0:T(8,128)(2,1)S(1)}) custom-call(s32[16]{0:T(128)S(1)} %copy-done.11, f32[1024,256]{1,0:T(8,128)S(1)} %get-tuple-element.123.grad_ref, f32[1024,256]{1,0:T(8,128)S(1)} %get-tuple-element.136.gm_ref, bf16[1024,256]{1,0:T(8,128)(2,1)S(1)} %copy-done.4, ...), custom_call_target="tpu_custom_call" | custom-call | flops 1000 | bytes 1024 | tf_op jit(solution)/shard_map/attn_bwd/pallas_call | solution.py:510
  116.3 5.1 %collective-permute-done.26.refs_4_ = bf16[432,256]{1,0:T(8,128)(2,1)S(1)} collective-permute-done((bf16[432,256]{1,0:T(8,128)(2,1)S(1)}, bf16[432,256]{1,0:T(8,128)(2,1)S(1)}, u32[]{:S(2)}, u32[]{:S(2)}) %collective-permute-start.26) | collective-permute-done | bytes 221216 | tf_op jit(solution)/shard_map/ppermute | solution.py:547
  121.4 0.1 four_sum.6.refs_0_
  121.5 1.3 collective-permute-start.27
  122.7 2.2 %collective-permute-start.33 = (bf16[688,256]{1,0:T(8,128)(2,1)S(1)}, bf16[688,256]{1,0:T(8,128)(2,1)S(1)}, u32[]{:S(2)}, u32[]{:S(2)}) collective-permute-start(bf16[688,256]{1,0:T(8,128)(2,1)S(1)} %four_sum.6.refs_0_), channel_id=1, source_target_pairs={{0,24},{4,28},{8,16},{12,20},{16,8},{20,12},{24,0},{28,4},{1,25},{... | collective-permute-start | bytes 1056776 | tf_op jit(solution)/shard_map/ppermute | solution.py:547
  124.9 0.2 collective-permute-start.32
  125.2 0.3 collective-permute-start.31
  125.4 0.1 core_sum.5
  125.6 1.4 collective-permute-start.29
  127.0 6.5 %collective-permute-done.33.refs_3_ = bf16[688,256]{1,0:T(8,128)(2,1)S(1)} collective-permute-done((bf16[688,256]{1,0:T(8,128)(2,1)S(1)}, bf16[688,256]{1,0:T(8,128)(2,1)S(1)}, u32[]{:S(2)}, u32[]{:S(2)}) %collective-permute-start.33) | collective-permute-done | bytes 352288 | tf_op jit(solution)/shard_map/ppermute | solution.py:547
  133.5 0.2 collective-permute-start.30
  133.7 4.1 %collective-permute-done.30.refs_3_ = bf16[176,256]{1,0:T(8,128)(2,1)S(1)} collective-permute-done((bf16[176,256]{1,0:T(8,128)(2,1)S(1)}, bf16[176,256]{1,0:T(8,128)(2,1)S(1)}, u32[]{:S(2)}, u32[]{:S(2)}) %collective-permute-start.30) | collective-permute-done | bytes 90144 | tf_op jit(solution)/shard_map/ppermute | solution.py:547
  137.8 3.6 %collective-permute-done.32.refs_2_ = bf16[688,256]{1,0:T(8,128)(2,1)S(1)} collective-permute-done((bf16[688,256]{1,0:T(8,128)(2,1)S(1)}, bf16[688,256]{1,0:T(8,128)(2,1)S(1)}, u32[]{:S(2)}, u32[]{:S(2)}) %collective-permute-start.32) | collective-permute-done | bytes 352288 | tf_op jit(solution)/shard_map/ppermute | solution.py:547
  141.4 0.2 four_sum.7.early
  141.6 0.6 collective-permute-start.34
  142.2 1.4 collective-permute-start.37
  143.7 1.0 collective-permute-start.36
  144.7 0.2 collective-permute-start.35
  145.0 2.5 %collective-permute-done.37.refs_3_ = bf16[176,256]{1,0:T(8,128)(2,1)S(1)} collective-permute-done((bf16[176,256]{1,0:T(8,128)(2,1)S(1)}, bf16[176,256]{1,0:T(8,128)(2,1)S(1)}, u32[]{:S(2)}, u32[]{:S(2)}) %collective-permute-start.37) | collective-permute-done | bytes 90144 | tf_op jit(solution)/shard_map/ppermute | solution.py:547
  147.4 2.3 %collective-permute-done.36.refs_2_ = bf16[176,256]{1,0:T(8,128)(2,1)S(1)} collective-permute-done((bf16[176,256]{1,0:T(8,128)(2,1)S(1)}, bf16[176,256]{1,0:T(8,128)(2,1)S(1)}, u32[]{:S(2)}, u32[]{:S(2)}) %collective-permute-start.36) | collective-permute-done | bytes 90144 | tf_op jit(solution)/shard_map/ppermute | solution.py:547
  149.8 0.5 collective-permute-start.38
  150.3 0.9 collective-permute-done.38.late_other
  151.2 1.3 finish.1
  (55 shorter events, 0.5 us)
Async XLA Ops:
  0.6 40.2 %copy-start.1 = (bf16[2,256,256]{2,1,0:T(8,128)(2,1)S(1)}, bf16[2,256,256]{2,1,0:T(8,128)(2,1)}, u32[]{:S(2)}) copy-start(bf16[2,256,256]{2,1,0:T(8,128)(2,1)} %down.7) | copy-start | bytes 786436
  0.7 40.2 %copy-start = (bf16[2,256,256]{2,1,0:T(8,128)(2,1)S(1)}, bf16[2,256,256]{2,1,0:T(8,128)(2,1)}, u32[]{:S(2)}) copy-start(bf16[2,256,256]{2,1,0:T(8,128)(2,1)} %up.7) | copy-start | bytes 786436
  0.7 40.2 %copy-start.10 = (f32[2,256]{1,0:T(2,128)S(1)}, f32[2,256]{1,0:T(2,128)}, u32[]{:S(2)}) copy-start(f32[2,256]{1,0:T(2,128)} %gain_ref.12) | copy-start | bytes 6148
  3.4 4.8 %collective-permute-start.2 = (bf16[176,256]{1,0:T(8,128)(2,1)}, bf16[176,256]{1,0:T(8,128)(2,1)S(1)}, u32[]{:S(2)}, u32[]{:S(2)}) collective-permute-start(bf16[176,256]{1,0:T(8,128)(2,1)} %get-tuple-element.89), channel_id=1, source_target_pairs={{0,3},{1,2},{2,1},{3,0},{4,7},{5,6},{6,5},{7,4},{8,11},{9,10},{10,... | collective-permute-start | bytes 270344 | tf_op jit(solution)/shard_map/ppermute | solution.py:547
  4.8 30.1 %collective-permute-start.6 = (bf16[432,256]{1,0:T(8,128)(2,1)}, bf16[432,256]{1,0:T(8,128)(2,1)S(1)}, u32[]{:S(2)}, u32[]{:S(2)}) collective-permute-start(bf16[432,256]{1,0:T(8,128)(2,1)} %get-tuple-element.92), channel_id=1, source_target_pairs={{0,1},{1,0},{2,3},{3,2},{4,5},{5,4},{6,7},{7,6},{8,9},{9,8},{10,11... | collective-permute-start | bytes 663560 | tf_op jit(solution)/shard_map/ppermute | solution.py:547
  7.0 8.1 %collective-permute-start.1 = (bf16[176,256]{1,0:T(8,128)(2,1)}, bf16[176,256]{1,0:T(8,128)(2,1)S(1)}, u32[]{:S(2)}, u32[]{:S(2)}) collective-permute-start(bf16[176,256]{1,0:T(8,128)(2,1)} %get-tuple-element.89), channel_id=1, source_target_pairs={{0,2},{1,3},{2,0},{3,1},{4,6},{5,7},{6,4},{7,5},{8,10},{9,11},{10,... | collective-permute-start | bytes 270344 | tf_op jit(solution)/shard_map/ppermute | solution.py:547
  7.0 10.8 %collective-permute-start = (bf16[176,256]{1,0:T(8,128)(2,1)}, bf16[176,256]{1,0:T(8,128)(2,1)S(1)}, u32[]{:S(2)}, u32[]{:S(2)}) collective-permute-start(bf16[176,256]{1,0:T(8,128)(2,1)} %get-tuple-element.89), channel_id=1, source_target_pairs={{0,1},{1,0},{2,3},{3,2},{4,5},{5,4},{6,7},{7,6},{8,9},{9,8},{10,11... | collective-permute-start | bytes 270344 | tf_op jit(solution)/shard_map/ppermute | solution.py:547
  8.3 12.3 %collective-permute-start.5 = (bf16[176,256]{1,0:T(8,128)(2,1)S(1)}, bf16[176,256]{1,0:T(8,128)(2,1)S(1)}, u32[]{:S(2)}, u32[]{:S(2)}) collective-permute-start(bf16[176,256]{1,0:T(8,128)(2,1)S(1)} %collective-permute-done.2.m3), channel_id=1, source_target_pairs={{0,4},{4,0},{8,12},{12,8},{16,20},{20,16},{24,28},{28,24},{1,5},{5... | collective-permute-start | bytes 270344 | tf_op jit(solution)/shard_map/ppermute | solution.py:547
  11.0 24.1 %collective-permute-start.8 = (bf16[432,256]{1,0:T(8,128)(2,1)}, bf16[432,256]{1,0:T(8,128)(2,1)S(1)}, u32[]{:S(2)}, u32[]{:S(2)}) collective-permute-start(bf16[432,256]{1,0:T(8,128)(2,1)} %get-tuple-element.92), channel_id=1, source_target_pairs={{0,3},{1,2},{2,1},{3,0},{4,7},{5,6},{6,5},{7,4},{8,11},{9,10},{10,... | collective-permute-start | bytes 663560 | tf_op jit(solution)/shard_map/ppermute | solution.py:547
  15.1 20.1 %collective-permute-start.7 = (bf16[432,256]{1,0:T(8,128)(2,1)}, bf16[432,256]{1,0:T(8,128)(2,1)S(1)}, u32[]{:S(2)}, u32[]{:S(2)}) collective-permute-start(bf16[432,256]{1,0:T(8,128)(2,1)} %get-tuple-element.92), channel_id=1, source_target_pairs={{0,2},{1,3},{2,0},{3,1},{4,6},{5,7},{6,4},{7,5},{8,10},{9,11},{10,... | collective-permute-start | bytes 663560 | tf_op jit(solution)/shard_map/ppermute | solution.py:547
  17.8 3.6 %collective-permute-start.4 = (bf16[176,256]{1,0:T(8,128)(2,1)S(1)}, bf16[176,256]{1,0:T(8,128)(2,1)S(1)}, u32[]{:S(2)}, u32[]{:S(2)}) collective-permute-start(bf16[176,256]{1,0:T(8,128)(2,1)S(1)} %collective-permute-done.1.m2), channel_id=1, source_target_pairs={{0,4},{4,0},{8,12},{12,8},{16,20},{20,16},{24,28},{28,24},{1,5},{5... | collective-permute-start | bytes 270344 | tf_op jit(solution)/shard_map/ppermute | solution.py:547
  20.5 1.3 collective-permute-start.3
  21.8 1.0 copy-start.3
  22.9 0.9 copy-start.5
  23.8 0.7 copy-start.8
  24.5 0.7 copy-start.11
  34.9 12.5 %copy-start.7 = (bf16[352,256]{1,0:T(8,128)(2,1)S(1)}, bf16[352,256]{1,0:T(8,128)(2,1)}, u32[]{:S(2)}) copy-start(bf16[352,256]{1,0:T(8,128)(2,1)} %get-tuple-element.97.own) | copy-start | bytes 540676
  34.9 5.9 %collective-permute-start.9 = (bf16[432,256]{1,0:T(8,128)(2,1)S(1)}, bf16[432,256]{1,0:T(8,128)(2,1)S(1)}, u32[]{:S(2)}, u32[]{:S(2)}) collective-permute-start(bf16[432,256]{1,0:T(8,128)(2,1)S(1)} %collective-permute-done.6.m1), channel_id=1, source_target_pairs={{0,4},{4,0},{8,12},{12,8},{16,20},{20,16},{24,28},{28,24},{1,5},{5... | collective-permute-start | bytes 663560 | tf_op jit(solution)/shard_map/ppermute | solution.py:547
  35.1 5.7 %collective-permute-start.10 = (bf16[432,256]{1,0:T(8,128)(2,1)S(1)}, bf16[432,256]{1,0:T(8,128)(2,1)S(1)}, u32[]{:S(2)}, u32[]{:S(2)}) collective-permute-start(bf16[432,256]{1,0:T(8,128)(2,1)S(1)} %collective-permute-done.7.m2), channel_id=1, source_target_pairs={{0,4},{4,0},{8,12},{12,8},{16,20},{20,16},{24,28},{28,24},{1,5},{5... | collective-permute-start | bytes 663560 | tf_op jit(solution)/shard_map/ppermute | solution.py:547
  35.5 5.3 %collective-permute-start.11 = (bf16[432,256]{1,0:T(8,128)(2,1)S(1)}, bf16[432,256]{1,0:T(8,128)(2,1)S(1)}, u32[]{:S(2)}, u32[]{:S(2)}) collective-permute-start(bf16[432,256]{1,0:T(8,128)(2,1)S(1)} %collective-permute-done.8.m3), channel_id=1, source_target_pairs={{0,4},{4,0},{8,12},{12,8},{16,20},{20,16},{24,28},{28,24},{1,5},{5... | collective-permute-start | bytes 663560 | tf_op jit(solution)/shard_map/ppermute | solution.py:547
  35.7 21.6 %collective-permute-start.14 = (bf16[256,256]{1,0:T(8,128)(2,1)}, bf16[256,256]{1,0:T(8,128)(2,1)S(1)}, u32[]{:S(2)}, u32[]{:S(2)}) collective-permute-start(bf16[256,256]{1,0:T(8,128)(2,1)} %get-tuple-element.100), channel_id=1, source_target_pairs={{0,3},{1,2},{2,1},{3,0},{4,7},{5,6},{6,5},{7,4},{8,11},{9,10},{10,... | collective-permute-start | bytes 393224 | tf_op jit(solution)/shard_map/ppermute | solution.py:547
  35.7 21.6 %collective-permute-start.13 = (bf16[256,256]{1,0:T(8,128)(2,1)}, bf16[256,256]{1,0:T(8,128)(2,1)S(1)}, u32[]{:S(2)}, u32[]{:S(2)}) collective-permute-start(bf16[256,256]{1,0:T(8,128)(2,1)} %get-tuple-element.100), channel_id=1, source_target_pairs={{0,2},{1,3},{2,0},{3,1},{4,6},{5,7},{6,4},{7,5},{8,10},{9,11},{10,... | collective-permute-start | bytes 393224 | tf_op jit(solution)/shard_map/ppermute | solution.py:547
  40.8 16.4 %collective-permute-start.12 = (bf16[256,256]{1,0:T(8,128)(2,1)}, bf16[256,256]{1,0:T(8,128)(2,1)S(1)}, u32[]{:S(2)}, u32[]{:S(2)}) collective-permute-start(bf16[256,256]{1,0:T(8,128)(2,1)} %get-tuple-element.100), channel_id=1, source_target_pairs={{0,1},{1,0},{2,3},{3,2},{4,5},{5,4},{6,7},{7,6},{8,9},{9,8},{10,11... | collective-permute-start | bytes 393224 | tf_op jit(solution)/shard_map/ppermute | solution.py:547
  47.4 12.4 %copy-start.2 = (bf16[1024,256]{1,0:T(8,128)(2,1)S(1)}, bf16[1024,256]{1,0:T(8,128)(2,1)}, u32[]{:S(2)}) copy-start(bf16[1024,256]{1,0:T(8,128)(2,1)} %grad_ref.1) | copy-start | bytes 1572868
  57.3 2.0 %collective-permute-start.15 = (bf16[256,256]{1,0:T(8,128)(2,1)S(1)}, bf16[256,256]{1,0:T(8,128)(2,1)S(1)}, u32[]{:S(2)}, u32[]{:S(2)}) collective-permute-start(bf16[256,256]{1,0:T(8,128)(2,1)S(1)} %collective-permute-done.12.m1), channel_id=1, source_target_pairs={{0,4},{4,0},{8,12},{12,8},{16,20},{20,16},{24,28},{28,24},{1,5},{5... | collective-permute-start | bytes 393224 | tf_op jit(solution)/shard_map/ppermute | solution.py:547
  58.2 1.3 collective-permute-start.16
  58.3 1.5 collective-permute-start.17
  59.8 15.3 %copy-start.9 = (f32[2,256]{1,0:T(2,128)S(1)}, f32[2,256]{1,0:T(2,128)}, u32[]{:S(2)}) copy-start(f32[2,256]{1,0:T(2,128)} %gain_ref.13) | copy-start | bytes 6148
  69.9 2.0 %collective-permute-start.18 = (bf16[4,256,256]{2,1,0:T(8,128)(2,1)S(1)}, bf16[4,256,256]{2,1,0:T(8,128)(2,1)S(1)}, u32[]{:S(2)}, u32[]{:S(2)}) collective-permute-start(bf16[4,256,256]{2,1,0:T(8,128)(2,1)S(1)} %get-tuple-element.107), channel_id=1, source_target_pairs={{0,4},{4,0},{8,12},{12,8},{16,20},{20,16},{24,28},{28,24},{1,5},{5... | collective-permute-start | bytes 1572872 | tf_op jit(solution)/shard_map/ppermute | solution.py:547
  72.0 16.7 %collective-permute-start.19 = (bf16[256,256]{1,0:T(8,128)(2,1)S(1)}, bf16[256,256]{1,0:T(8,128)(2,1)S(1)}, u32[]{:S(2)}, u32[]{:S(2)}) collective-permute-start(bf16[256,256]{1,0:T(8,128)(2,1)S(1)} %get-tuple-element.109), channel_id=1, source_target_pairs={{0,1},{1,0},{2,3},{3,2},{4,5},{5,4},{6,7},{7,6},{8,9},{9,8},{10,11... | collective-permute-start | bytes 393224 | tf_op jit(solution)/shard_map/ppermute | solution.py:547
  73.8 14.9 %collective-permute-start.20 = (bf16[256,256]{1,0:T(8,128)(2,1)S(1)}, bf16[256,256]{1,0:T(8,128)(2,1)S(1)}, u32[]{:S(2)}, u32[]{:S(2)}) collective-permute-start(bf16[256,256]{1,0:T(8,128)(2,1)S(1)} %get-tuple-element.110), channel_id=1, source_target_pairs={{0,2},{1,3},{2,0},{3,1},{4,6},{5,7},{6,4},{7,5},{8,10},{9,11},{10,... | collective-permute-start | bytes 393224 | tf_op jit(solution)/shard_map/ppermute | solution.py:547
  73.8 14.9 %collective-permute-start.21 = (bf16[256,256]{1,0:T(8,128)(2,1)S(1)}, bf16[256,256]{1,0:T(8,128)(2,1)S(1)}, u32[]{:S(2)}, u32[]{:S(2)}) collective-permute-start(bf16[256,256]{1,0:T(8,128)(2,1)S(1)} %get-tuple-element.111), channel_id=1, source_target_pairs={{0,3},{1,2},{2,1},{3,0},{4,7},{5,6},{6,5},{7,4},{8,11},{9,10},{10,... | collective-permute-start | bytes 393224 | tf_op jit(solution)/shard_map/ppermute | solution.py:547
  88.8 13.1 %copy-start.6 = (bf16[352,256]{1,0:T(8,128)(2,1)S(1)}, bf16[352,256]{1,0:T(8,128)(2,1)}, u32[]{:S(2)}) copy-start(bf16[352,256]{1,0:T(8,128)(2,1)} %get-tuple-element.88.own) | copy-start | bytes 540676
  94.8 7.1 %copy-start.4 = (bf16[1024,256]{1,0:T(8,128)(2,1)S(1)}, bf16[1024,256]{1,0:T(8,128)(2,1)}, u32[]{:S(2)}) copy-start(bf16[1024,256]{1,0:T(8,128)(2,1)} %cur_ref.3) | copy-start | bytes 1572868
  94.8 3.0 %collective-permute-start.23 = (bf16[4,256,256]{2,1,0:T(8,128)(2,1)S(1)}, bf16[4,256,256]{2,1,0:T(8,128)(2,1)S(1)}, u32[]{:S(2)}, u32[]{:S(2)}) collective-permute-start(bf16[4,256,256]{2,1,0:T(8,128)(2,1)S(1)} %get-tuple-element.131), channel_id=1, source_target_pairs={{0,4},{4,0},{8,12},{12,8},{16,20},{20,16},{24,28},{28,24},{1,5},{5... | collective-permute-start | bytes 1572872 | tf_op jit(solution)/shard_map/ppermute | solution.py:547
  95.7 2.1 %collective-permute-start.22 = (bf16[4,176,256]{2,1,0:T(8,128)(2,1)S(1)}, bf16[4,176,256]{2,1,0:T(8,128)(2,1)S(1)}, u32[]{:S(2)}, u32[]{:S(2)}) collective-permute-start(bf16[4,176,256]{2,1,0:T(8,128)(2,1)S(1)} %get-tuple-element.128), channel_id=1, source_target_pairs={{0,4},{4,0},{8,12},{12,8},{16,20},{20,16},{24,28},{28,24},{1,5},{5... | collective-permute-start | bytes 1081352 | tf_op jit(solution)/shard_map/ppermute | solution.py:547
  98.0 18.3 %collective-permute-start.24 = (bf16[432,256]{1,0:T(8,128)(2,1)S(1)}, bf16[432,256]{1,0:T(8,128)(2,1)S(1)}, u32[]{:S(2)}, u32[]{:S(2)}) collective-permute-start(bf16[432,256]{1,0:T(8,128)(2,1)S(1)} %get-tuple-element.133), channel_id=1, source_target_pairs={{0,1},{1,0},{2,3},{3,2},{4,5},{5,4},{6,7},{7,6},{8,9},{9,8},{10,11... | collective-permute-start | bytes 663560 | tf_op jit(solution)/shard_map/ppermute | solution.py:547
  100.6 15.6 %collective-permute-start.25 = (bf16[432,256]{1,0:T(8,128)(2,1)S(1)}, bf16[432,256]{1,0:T(8,128)(2,1)S(1)}, u32[]{:S(2)}, u32[]{:S(2)}) collective-permute-start(bf16[432,256]{1,0:T(8,128)(2,1)S(1)} %get-tuple-element.134), channel_id=1, source_target_pairs={{0,2},{1,3},{2,0},{3,1},{4,6},{5,7},{6,4},{7,5},{8,10},{9,11},{10,... | collective-permute-start | bytes 663560 | tf_op jit(solution)/shard_map/ppermute | solution.py:547
  100.7 20.7 %collective-permute-start.26 = (bf16[432,256]{1,0:T(8,128)(2,1)S(1)}, bf16[432,256]{1,0:T(8,128)(2,1)S(1)}, u32[]{:S(2)}, u32[]{:S(2)}) collective-permute-start(bf16[432,256]{1,0:T(8,128)(2,1)S(1)} %get-tuple-element.135), channel_id=1, source_target_pairs={{0,3},{1,2},{2,1},{3,0},{4,7},{5,6},{6,5},{7,4},{8,11},{9,10},{10,... | collective-permute-start | bytes 663560 | tf_op jit(solution)/shard_map/ppermute | solution.py:547
  121.5 3.9 %collective-permute-start.27 = (bf16[4,176,256]{2,1,0:T(8,128)(2,1)S(1)}, bf16[4,176,256]{2,1,0:T(8,128)(2,1)S(1)}, u32[]{:S(2)}, u32[]{:S(2)}) collective-permute-start(bf16[4,176,256]{2,1,0:T(8,128)(2,1)S(1)} %get-tuple-element.149), channel_id=1, source_target_pairs={{0,4},{4,0},{8,12},{12,8},{16,20},{20,16},{24,28},{28,24},{1,5},{5... | collective-permute-start | bytes 1081352 | tf_op jit(solution)/shard_map/ppermute | solution.py:547
  122.7 10.8 %collective-permute-start.33 = (bf16[688,256]{1,0:T(8,128)(2,1)S(1)}, bf16[688,256]{1,0:T(8,128)(2,1)S(1)}, u32[]{:S(2)}, u32[]{:S(2)}) collective-permute-start(bf16[688,256]{1,0:T(8,128)(2,1)S(1)} %four_sum.6.refs_0_), channel_id=1, source_target_pairs={{0,24},{4,28},{8,16},{12,20},{16,8},{20,12},{24,0},{28,4},{1,25},{... | collective-permute-start | bytes 1056776 | tf_op jit(solution)/shard_map/ppermute | solution.py:547
  124.9 16.5 %collective-permute-start.32 = (bf16[688,256]{1,0:T(8,128)(2,1)S(1)}, bf16[688,256]{1,0:T(8,128)(2,1)S(1)}, u32[]{:S(2)}, u32[]{:S(2)}) collective-permute-start(bf16[688,256]{1,0:T(8,128)(2,1)S(1)} %four_sum.6.refs_0_), channel_id=1, source_target_pairs={{0,16},{4,20},{8,24},{12,28},{16,0},{20,4},{24,8},{28,12},{1,17},{... | collective-permute-start | bytes 1056776 | tf_op jit(solution)/shard_map/ppermute | solution.py:547
  125.2 16.2 %collective-permute-start.31 = (bf16[688,256]{1,0:T(8,128)(2,1)S(1)}, bf16[688,256]{1,0:T(8,128)(2,1)S(1)}, u32[]{:S(2)}, u32[]{:S(2)}) collective-permute-start(bf16[688,256]{1,0:T(8,128)(2,1)S(1)} %four_sum.6.refs_0_), channel_id=1, source_target_pairs={{0,8},{4,12},{8,0},{12,4},{16,24},{20,28},{24,16},{28,20},{1,9},{5... | collective-permute-start | bytes 1056776 | tf_op jit(solution)/shard_map/ppermute | solution.py:547
  125.5 8.2 %collective-permute-start.28 = (bf16[176,256]{1,0:T(8,128)(2,1)S(1)}, bf16[176,256]{1,0:T(8,128)(2,1)S(1)}, u32[]{:S(2)}, u32[]{:S(2)}) collective-permute-start(bf16[176,256]{1,0:T(8,128)(2,1)S(1)} %get-tuple-element.150), channel_id=1, source_target_pairs={{0,1},{1,0},{2,3},{3,2},{4,5},{5,4},{6,7},{7,6},{8,9},{9,8},{10,11... | collective-permute-start | bytes 270344 | tf_op jit(solution)/shard_map/ppermute | solution.py:547
  125.6 8.1 %collective-permute-start.29 = (bf16[176,256]{1,0:T(8,128)(2,1)S(1)}, bf16[176,256]{1,0:T(8,128)(2,1)S(1)}, u32[]{:S(2)}, u32[]{:S(2)}) collective-permute-start(bf16[176,256]{1,0:T(8,128)(2,1)S(1)} %get-tuple-element.151), channel_id=1, source_target_pairs={{0,2},{1,3},{2,0},{3,1},{4,6},{5,7},{6,4},{7,5},{8,10},{9,11},{10,... | collective-permute-start | bytes 270344 | tf_op jit(solution)/shard_map/ppermute | solution.py:547
  133.5 4.3 %collective-permute-start.30 = (bf16[176,256]{1,0:T(8,128)(2,1)S(1)}, bf16[176,256]{1,0:T(8,128)(2,1)S(1)}, u32[]{:S(2)}, u32[]{:S(2)}) collective-permute-start(bf16[176,256]{1,0:T(8,128)(2,1)S(1)} %get-tuple-element.152), channel_id=1, source_target_pairs={{0,3},{1,2},{2,1},{3,0},{4,7},{5,6},{6,5},{7,4},{8,11},{9,10},{10,... | collective-permute-start | bytes 270344 | tf_op jit(solution)/shard_map/ppermute | solution.py:547
  141.6 9.7 %collective-permute-start.34 = (bf16[688,256]{1,0:T(8,128)(2,1)S(1)}, bf16[688,256]{1,0:T(8,128)(2,1)S(1)}, u32[]{:S(2)}, u32[]{:S(2)}) collective-permute-start(bf16[688,256]{1,0:T(8,128)(2,1)S(1)} %four_sum.7.early), channel_id=1, source_target_pairs={{0,4},{4,0},{8,12},{12,8},{16,20},{20,16},{24,28},{28,24},{1,5},{5... | collective-permute-start | bytes 1056776 | tf_op jit(solution)/shard_map/ppermute | solution.py:547
  142.2 5.2 %collective-permute-start.37 = (bf16[176,256]{1,0:T(8,128)(2,1)S(1)}, bf16[176,256]{1,0:T(8,128)(2,1)S(1)}, u32[]{:S(2)}, u32[]{:S(2)}) collective-permute-start(bf16[176,256]{1,0:T(8,128)(2,1)S(1)} %four_sum.8.refs_0_), channel_id=1, source_target_pairs={{0,24},{4,28},{8,16},{12,20},{16,8},{20,12},{24,0},{28,4},{1,25},{... | collective-permute-start | bytes 270344 | tf_op jit(solution)/shard_map/ppermute | solution.py:547
  143.7 6.0 %collective-permute-start.36 = (bf16[176,256]{1,0:T(8,128)(2,1)S(1)}, bf16[176,256]{1,0:T(8,128)(2,1)S(1)}, u32[]{:S(2)}, u32[]{:S(2)}) collective-permute-start(bf16[176,256]{1,0:T(8,128)(2,1)S(1)} %four_sum.8.refs_0_), channel_id=1, source_target_pairs={{0,16},{4,20},{8,24},{12,28},{16,0},{20,4},{24,8},{28,12},{1,17},{... | collective-permute-start | bytes 270344 | tf_op jit(solution)/shard_map/ppermute | solution.py:547
  144.7 5.0 %collective-permute-start.35 = (bf16[176,256]{1,0:T(8,128)(2,1)S(1)}, bf16[176,256]{1,0:T(8,128)(2,1)S(1)}, u32[]{:S(2)}, u32[]{:S(2)}) collective-permute-start(bf16[176,256]{1,0:T(8,128)(2,1)S(1)} %four_sum.8.refs_0_), channel_id=1, source_target_pairs={{0,8},{4,12},{8,0},{12,4},{16,24},{20,28},{24,16},{28,20},{1,9},{5... | collective-permute-start | bytes 270344 | tf_op jit(solution)/shard_map/ppermute | solution.py:547
  149.8 1.5 collective-permute-start.38
